TPU v7x, 32 devices: a whole 2x2x4 slice. The times are simulated.
32 devices in a mesh: dp: 4 (over y, x), hid: 4 (over z), mod: 2 (over core).
Axes of the slice: x: 2, y: 2, z: 4, core: 2. Of those that a mesh axis runs over, the one named last changes fastest.
Arguments:
- tokens: bfloat16 [32768, 768], P(('dp', 'hid', 'mod')), may hold values from -6 to 6
- clusters: int32 [32768, 12], P(('dp', 'hid', 'mod')), may hold values from 0 to 99
- key_mask: int32 [32768], P(('dp', 'hid', 'mod')), may hold values from 0 to 1, as said below
- query_key_value_weight: bfloat16 [768, 2304], replicated, may hold values from -0.5 to 0.5
- attention_output_weight: bfloat16 [768, 768], replicated, may hold values from -0.4375 to 0.4375
- up_weight: bfloat16 [768, 3072], P('mod', 'hid'), may hold values from -0.21875 to 0.21875
- down_weight: bfloat16 [3072, 768], P('hid', 'mod'), may hold values from -0.109375 to 0.109375
- gain_one: float32 [768], replicated, may hold values from 0.1 to 1.9
- shift_one: float32 [768], replicated, may hold values from -3 to 3
- gain_two: float32 [768], replicated, may hold values from 0.1 to 1.9
- shift_two: float32 [768], replicated, may hold values from -3 to 3
- cotangent: bfloat16 [32768, 768], P(('dp', 'hid', 'mod')), may hold values from -6 to 6
Outputs:
- output: bfloat16 [32768, 768], P(('dp', 'hid', 'mod'))
- input_grad: bfloat16 [32768, 768], P(('dp', 'hid', 'mod'))
- grad_qkv: float32 [768, 2304], replicated
- grad_out: float32 [768, 768], replicated
- grad_in: float32 [768, 3072], P('mod', 'hid')
- grad_back: float32 [3072, 768], P('hid', 'mod')
- grad_gain_one: float32 [768], replicated
- grad_shift_one: float32 [768], replicated
- grad_gain_two: float32 [768], replicated
- grad_shift_two: float32 [768], replicated
Inputs may be any that keep to these rules, and one draw needn't show every extreme that they name: `key_mask`: the first position of each sequence of 1024 tokens is always 1.
All inputs are finite; a program needn't handle non-finite values.
Results may differ from a plain program's by a relative error of at most 0.019.
Values may be sent and summed in bfloat16 or wider, within the bound.
No kernel may reach another device: no remote copies, remote signals or barrier semaphores. Data moves between devices by JAX's collectives and lax.ppermute only.
A program may use at most 192 MiB of HBM per device.

v0:
```python
import jax
import jax.numpy as jnp
from jax import lax
from jax.sharding import PartitionSpec as P

H = 12
DH = 64
C = 100
LEN = 1024


EPSILON = 1e-05
NEGATIVE = -1e30
FULL_PRECISION = lax.Precision.HIGHEST


def normalize(inputs, gain_vec, shift_vec):
    row_mean = jnp.mean(inputs, axis=-1, keepdims=True)
    centered = inputs - row_mean
    row_var = jnp.mean(centered * centered, axis=-1, keepdims=True)
    return centered * lax.rsqrt(row_var + EPSILON) * gain_vec + shift_vec


def exact_gelu(inputs):
    return jax.nn.gelu(inputs, approximate=False)


def per_device(
    tokens,
    clusters,
    key_mask,
    query_key_value_weight,
    attention_output_weight,
    up_weight,
    down_weight,
    gain_one,
    shift_one,
    gain_two,
    shift_two,
    cotangent,
):
    tok_rows, model_width = tokens.shape
    seq_count = tok_rows // LEN
    head_scale = DH ** (-0.5)
    inputs = tokens.astype(jnp.float32)
    first_normalized_input, norm_one_back = jax.vjp(normalize, inputs, gain_one, shift_one)
    normed_low = first_normalized_input.astype(jnp.bfloat16)
    output_projected = jnp.dot(
        normed_low, query_key_value_weight, preferred_element_type=jnp.float32
    ).astype(jnp.bfloat16)
    output_projected = output_projected.reshape(seq_count, LEN, 3, H, DH)
    query = output_projected[:, :, 0]
    key_part = output_projected[:, :, 1]
    value_part = output_projected[:, :, 2]
    member_test = clusters.reshape(seq_count, LEN, H, 1) == jnp.arange(C, dtype=jnp.int32)
    member = member_test.astype(jnp.bfloat16)
    counts = jnp.maximum(jnp.sum(member_test.astype(jnp.float32), axis=1), 1.0)
    summed = jnp.einsum("slhc,slhd->shcd", member, query, preferred_element_type=jnp.float32)
    centre = (summed / counts[..., None]).astype(jnp.bfloat16)
    keep_mask = key_mask.reshape(seq_count, 1, 1, LEN) == 1

    def score_block():
        raw_scores = (
            jnp.einsum("shcd,slhd->shcl", centre, key_part, preferred_element_type=jnp.float32)
            * head_scale
        )
        return jnp.where(keep_mask, raw_scores, NEGATIVE)

    scores = score_block()
    top_score = jnp.max(scores, axis=-1, keepdims=True)
    powered = jnp.exp(scores - top_score)
    row_total = jnp.sum(powered, axis=-1, keepdims=True)
    log_total = top_score + jnp.log(row_total)
    prob_low = (powered / row_total).astype(jnp.bfloat16)
    centre_out = jnp.einsum(
        "shcl,slhd->shcd", prob_low, value_part, preferred_element_type=jnp.float32
    )
    centre_out = centre_out.astype(jnp.bfloat16)
    attention_mixture = jnp.einsum(
        "slhc,shcd->slhd", member, centre_out, preferred_element_type=jnp.float32
    )
    attention_mixture = attention_mixture.astype(jnp.bfloat16).reshape(tok_rows, model_width)
    attention_result = jnp.dot(
        attention_mixture, attention_output_weight, preferred_element_type=jnp.float32
    )
    residual_stream = inputs + attention_result
    second_normalized_input, norm_two_back = jax.vjp(
        normalize, residual_stream, gain_two, shift_two
    )
    normed_two_low = second_normalized_input.astype(jnp.bfloat16)
    cot_float = cotangent.astype(jnp.float32)
    local_in, local_back = (
        lax.all_gather(up_weight, "mod", axis=0, tiled=True),
        lax.all_gather(down_weight, "mod", axis=1, tiled=True),
    )
    rows_all = lax.all_gather(normed_two_low, "hid", axis=0, tiled=True)
    hidden_before_activation = jnp.dot(rows_all, local_in, preferred_element_type=jnp.float32)
    hidden_activation, gelu_back = jax.vjp(exact_gelu, hidden_before_activation)
    act_low = hidden_activation.astype(jnp.bfloat16)
    piece = act_low
    branch = lax.psum_scatter(
        jnp.dot(piece, local_back, preferred_element_type=jnp.float32).astype(jnp.bfloat16),
        "hid",
        scatter_dimension=0,
        tiled=True,
    ).astype(jnp.float32)
    output = (residual_stream + branch).astype(jnp.bfloat16)
    cot_all = lax.all_gather(cotangent, "hid", axis=0, tiled=True)
    back_full = jnp.einsum("tf,td->fd", act_low, cot_all, preferred_element_type=jnp.float32)
    grad_act = jnp.einsum("td,fd->tf", cot_all, local_back, preferred_element_type=jnp.float32)
    grad_pre = gelu_back(grad_act)[0].astype(jnp.bfloat16)
    in_full = jnp.einsum("td,tf->df", rows_all, grad_pre, preferred_element_type=jnp.float32)
    piece = grad_pre
    grad_normed_two = lax.psum_scatter(
        jnp.einsum("tf,df->td", piece, local_in, preferred_element_type=jnp.float32).astype(
            jnp.bfloat16
        ),
        "hid",
        scatter_dimension=0,
        tiled=True,
    ).astype(jnp.float32)
    part_in, part_back = (
        lax.psum_scatter(
            in_full.astype(jnp.bfloat16), "mod", scatter_dimension=0, tiled=True
        ).astype(jnp.float32),
        lax.psum_scatter(
            back_full.astype(jnp.bfloat16), "mod", scatter_dimension=1, tiled=True
        ).astype(jnp.float32),
    )
    grad_in_sum, grad_back_sum = (
        lax.psum(part_in.astype(jnp.bfloat16), "dp").astype(jnp.float32),
        lax.psum(part_back.astype(jnp.bfloat16), "dp").astype(jnp.float32),
    )
    grad_resid_norm, grad_gain_two, grad_shift_two = norm_two_back(grad_normed_two)
    grad_residual = cot_float + grad_resid_norm
    grad_attended = grad_residual.astype(jnp.bfloat16)
    grad_wout = jnp.einsum(
        "td,te->de", attention_mixture, grad_attended, preferred_element_type=jnp.float32
    )
    grad_mixed = jnp.einsum(
        "te,de->td", grad_attended, attention_output_weight, preferred_element_type=jnp.float32
    )
    grad_mixed = grad_mixed.astype(jnp.bfloat16).reshape(seq_count, LEN, H, DH)
    grad_centre_out = jnp.einsum(
        "slhc,slhd->shcd", member, grad_mixed, preferred_element_type=jnp.float32
    )
    grad_centre_out = grad_centre_out.astype(jnp.bfloat16)
    probability = jnp.exp(score_block() - log_total)
    grad_prob = jnp.einsum(
        "shcd,slhd->shcl", grad_centre_out, value_part, preferred_element_type=jnp.float32
    )
    grad_value = jnp.einsum(
        "shcl,shcd->slhd", prob_low, grad_centre_out, preferred_element_type=jnp.float32
    )
    inner_sum = jnp.sum(probability * grad_prob, axis=-1, keepdims=True)
    grad_scores = (probability * (grad_prob - inner_sum)).astype(jnp.bfloat16)
    grad_centre = (
        jnp.einsum("shcl,slhd->shcd", grad_scores, key_part, preferred_element_type=jnp.float32)
        * head_scale
    )
    grad_centre = grad_centre.astype(jnp.bfloat16)
    grad_key = (
        jnp.einsum("shcl,shcd->slhd", grad_scores, centre, preferred_element_type=jnp.float32)
        * head_scale
    )
    picked = jnp.einsum("slhc,shcd->slhd", member, grad_centre, preferred_element_type=jnp.float32)
    count_each = jnp.einsum(
        "slhc,shc->slh", member_test.astype(jnp.float32), counts, precision=FULL_PRECISION
    )
    grad_query = picked / count_each[..., None]
    grad_projected = jnp.stack([grad_query, grad_key, grad_value], axis=2)
    grad_projected = grad_projected.reshape(tok_rows, 3 * model_width).astype(jnp.bfloat16)
    grad_wqkv = jnp.einsum(
        "td,te->de", normed_low, grad_projected, preferred_element_type=jnp.float32
    )
    grad_normed_one = jnp.einsum(
        "te,de->td", grad_projected, query_key_value_weight, preferred_element_type=jnp.float32
    )
    grad_input_norm, grad_gain_one, grad_shift_one = norm_one_back(grad_normed_one)
    input_grad = (grad_residual + grad_input_norm).astype(jnp.bfloat16)
    summed_grads = lax.psum(
        (grad_wqkv, grad_wout, grad_gain_one, grad_shift_one, grad_gain_two, grad_shift_two),
        ("dp", "hid", "mod"),
    )
    return (
        output,
        input_grad,
        summed_grads[0],
        summed_grads[1],
        grad_in_sum,
        grad_back_sum,
        summed_grads[2],
        summed_grads[3],
        summed_grads[4],
        summed_grads[5],
    )


def solution(mesh):
    placed = (
        P(("dp", "hid", "mod"), None),
        P(("dp", "hid", "mod"), None),
        P(("dp", "hid", "mod")),
        P(),
        P(),
        P("mod", "hid"),
        P("hid", "mod"),
        P(),
        P(),
        P(),
        P(),
        P(("dp", "hid", "mod"), None),
    )
    return jax.shard_map(
        per_device,
        mesh=mesh,
        in_specs=placed,
        out_specs=(
            P(("dp", "hid", "mod"), None),
            P(("dp", "hid", "mod"), None),
            P(),
            P(),
            P("mod", "hid"),
            P("hid", "mod"),
            P(),
            P(),
            P(),
            P(),
        ),
        check_vma=False,
    )
```

profile of v0, /device:TPU:0, one launch (start us, length us, event | category | flops | bytes accessed | tf_op | source)
XLA Modules:
  0.0 880.6 jit_solution(3841330076981364218)
XLA Ops:
  8.9 8.4 fusion.11
  17.9 2.8 copy.54
  20.7 1.8 convert_reduce_fusion.1
  22.5 1.9 fusion.25
  25.6 5.8 convolution_convert_fusion.2
  31.4 6.6 copy.55
  38.0 2.5 fusion.49
  40.5 2.5 fusion.29
  45.9 2.4 divide_convert_fusion
  48.4 5.6 fusion.36
  53.9 3.8 fusion.62
  63.0 116.9 %all-gather.5.cloned.1.call-done = bf16[4096,768]{0,1:T(8,128)(2,1)} async-done(((bf16[1024,768]{0,1:T(8,128)(2,1)}), bf16[4096,768]{0,1:T(8,128)(2,1)}) %all-gather.5.cloned.1.call-update) | async-done | bytes 6291472 | tf_op jit(solution)/shard_map/all_gather | solution.py:96
  179.9 10.6 %fusion.64 = f32[4096,768]{1,0:T(8,128)} fusion(bf16[4096,768]{0,1:T(8,128)(2,1)} %all-gather.5.cloned.1.call-done, bf16[768,768]{1,0:T(8,128)(2,1)} %all-gather.7.cloned.1.call-done), kind=kOutput, calls=%fused_computation.118 | convolution fusion | flops 4831838208 | bytes 20054016 | tf_op jit(solution)/shard_map/dot_general | solution.py:97
  190.5 116.4 %all-gather.11.cloned.1.call-done = bf16[4096,768]{1,0:T(8,128)(2,1)} async-done(((bf16[1024,768]{1,0:T(8,128)(2,1)}), bf16[4096,768]{1,0:T(8,128)(2,1)}) %all-gather.11.cloned.1.call-update) | async-done | bytes 6291472 | tf_op jit(solution)/shard_map/all_gather | solution.py:108
  306.9 35.5 %add_convert_fusion = (bf16[4096,768]{1,0:T(8,128)(2,1)}, f32[4096,768]{1,0:T(8,128)S(1)}) fusion(f32[4096,768]{1,0:T(8,128)} %fusion.64, bf16[4096,768]{1,0:T(8,128)(2,1)} %all-gather.11.cloned.1.call-done, bf16[768,768]{1,0:T(8,128)(2,1)} %all-gather.9.cloned.1.call-done), kind=kOutput, calls=%fused_computation.3 | convolution fusion | flops 5058330624 | bytes 38928384 | tf_op jit(solution)/shard_map/td,fd->tf/dot_general | solution.py:110
  342.4 4.3 multiply_convert_fusion
  346.7 9.9 %convolution_convert_fusion.5 = bf16[768,768]{1,0:T(8,128)(2,1)} fusion(bf16[4096,768]{1,0:T(8,128)(2,1)} %multiply_convert_fusion, bf16[4096,768]{1,0:T(8,128)(2,1)} %all-gather.11.cloned.1.call-done), kind=kOutput, calls=%fused_computation.80 | convolution fusion | flops 4832428032 | bytes 13762560 | tf_op jit(solution)/shard_map/tf,td->fd/dot_general | solution.py:109
  356.6 2.4 copy.67
  359.0 9.8 %convolution_convert_fusion.6 = bf16[768,768]{1,0:T(8,128)(2,1)} fusion(bf16[4096,768]{0,1:T(8,128)(2,1)} %all-gather.5.cloned.1.call-done, bf16[4096,768]{1,0:T(8,128)(2,1)} %get-tuple-element.64), kind=kOutput, calls=%fused_computation.81 | convolution fusion | flops 4832428032 | bytes 13762560 | tf_op jit(solution)/shard_map/td,tf->df/dot_general | solution.py:112
  368.9 9.4 %convolution_convert_fusion = bf16[4096,768]{0,1:T(8,128)(2,1)} fusion(bf16[4096,768]{1,0:T(8,128)(2,1)} %get-tuple-element.64, bf16[768,768]{1,0:T(8,128)(2,1)} %all-gather.7.cloned.1.call-done), kind=kOutput, calls=%fused_computation.18 | convolution fusion | flops 4834983936 | bytes 13762560 | tf_op jit(solution)/shard_map/tf,df->td/dot_general | solution.py:115
  378.4 2.1 copy.68
  380.6 9.2 %convolution_convert_fusion.1 = bf16[4096,768]{0,1:T(8,128)(2,1)} fusion(bf16[4096,768]{1,0:T(8,128)(2,1)} %multiply_convert_fusion, bf16[768,768]{1,0:T(8,128)(2,1)} %all-gather.9.cloned.1.call-done), kind=kOutput, calls=%fused_computation.19 | convolution fusion | flops 4834983936 | bytes 13762560 | tf_op jit(solution)/shard_map/dot_general | solution.py:102
  389.9 2.6 copy.57
  392.5 2.5 fusion.6
  397.0 95.9 %reduce-scatter.9.cloned.1.call-done = bf16[1024,768]{0,1:T(8,128)(2,1)} async-done(((bf16[4096,768]{0,1:T(8,128)(2,1)}), bf16[1024,768]{0,1:T(8,128)(2,1)}) %reduce-scatter.9.cloned.1.call-update) | async-done | bytes 1572880 | tf_op jit(solution)/shard_map/reduce_scatter | solution.py:114
  493.0 4.1 convert_reduce_fusion
  497.1 2.2 fusion.27
  505.0 2.0 fusion.37
  507.0 3.1 multiply_reduce_fusion
  513.2 1.8 fusion.38
  515.0 5.6 fusion.39
  520.6 2.8 pad_maximum_fusion
  524.0 2.8 fusion.65
  526.9 6.3 fusion.57
  533.3 18.6 %all-reduce.8.cloned.1.call-done = (bf16[384,768]{1,0:T(8,128)(2,1)}, bf16[768,384]{1,0:T(8,128)(2,1)}) async-done(((bf16[384,768]{1,0:T(8,128)(2,1)}, bf16[768,384]{1,0:T(8,128)(2,1)}), (bf16[384,768]{1,0:T(8,128)(2,1)}, bf16[768,384]{1,0:T(8,128)(2,1)})) %all-reduce.8.cloned.1.call-update) | async-done | bytes 1179664 | tf_op jit(solution)/shard_map/psum | solution.py:131
  551.9 2.2 convert_element_type.138
  554.0 2.2 convert_element_type.140
  556.2 8.4 fusion.63
  564.6 3.7 copy.59
  568.4 3.0 fusion.26
  572.2 1.9 fusion.23
  574.7 90.3 %reduce-scatter.7.cloned.1.call-done = bf16[1024,768]{0,1:T(8,128)(2,1)} async-done(((bf16[4096,768]{0,1:T(8,128)(2,1)}), bf16[1024,768]{0,1:T(8,128)(2,1)}) %reduce-scatter.7.cloned.1.call-update) | async-done | bytes 1572880 | tf_op jit(solution)/shard_map/reduce_scatter | solution.py:101
  665.1 7.1 add_convert_fusion.1
  672.2 2.6 copy.62
  674.8 2.6 copy.61
  677.4 43.1 %all-reduce = (f32[768]{0:T(1024)}, f32[768]{0:T(1024)}, f32[768]{0:T(1024)}, f32[768]{0:T(1024)}) all-reduce(f32[768]{0:T(1024)S(1)} %copy-done.49, f32[768]{0:T(1024)S(1)} %copy-done.51, f32[768]{0:T(1024)S(1)} %copy-done.48, f32[768]{0:T(1024)S(1)} %copy-done.47), channel_id=1, replica_groups=mesh['dp'=4,'hid'=4,'mod'=2] {'dp','hid','mod'}, use_global_device_ids=true, to_apply=%region_21.22 | all-reduce | flops 3072 | bytes 24576 | tf_op jit(solution)/shard_map/psum | solution.py:181
  720.6 144.7 %all-reduce.6.cloned.1.call-done = (f32[768,2304]{1,0:T(8,128)}, f32[768,768]{1,0:T(8,128)}) async-done(((f32[768,2304]{1,0:T(8,128)}, f32[768,768]{1,0:T(8,128)}), (f32[768,2304]{1,0:T(8,128)}, f32[768,768]{1,0:T(8,128)})) %all-reduce.6.cloned.1.call-update) | async-done | bytes 9437200 | tf_op jit(solution)/shard_map/psum | solution.py:181
  865.3 6.6 copy.77
  (161 shorter events, 26.0 us)
Async XLA Ops:
  7.2 18.4 %copy-start = (bf16[768,2304]{1,0:T(8,128)(2,1)S(1)}, bf16[768,2304]{1,0:T(8,128)(2,1)}, u32[]{:S(2)}) copy-start(bf16[768,2304]{1,0:T(8,128)(2,1)} %param.15) | copy-start | bytes 10616836
  7.2 55.8 %all-gather.7.cloned.1.call-start = ((), (), s32[]{:S(2)}) async-start(), calls=%async_computation.5 | async-start | bytes 1769472 | tf_op jit(solution)/shard_map/all_gather | solution.py:93
  7.9 172.0 %all-gather.5.cloned.1.call-start = ((), (), s32[]{:S(2)}) async-start(), calls=%async_computation.4 | async-start | bytes 7864320 | tf_op jit(solution)/shard_map/all_gather | solution.py:96
  8.9 35.3 %copy-start.45 = (pred[1024]{0:T(1024)(128)(4,1)}, pred[1024]{0:T(1024)(128)(4,1)S(1)}, u32[]{:S(2)}) copy-start(pred[1024]{0:T(1024)(128)(4,1)S(1)} %broadcast_compare_fusion) | copy-start | bytes 3076
  17.9 7.7 copy-start.42
  20.7 4.9 copy-start.4
  20.7 4.9 copy-start.53
  22.5 2.5 copy-start.27
  40.5 2.5 copy-start.17
  61.6 128.9 %all-gather.9.cloned.1.call-start = ((), (), s32[]{:S(2)}) async-start(), calls=%async_computation.6 | async-start | bytes 1769472 | tf_op jit(solution)/shard_map/all_gather | solution.py:94
  62.4 244.5 %all-gather.11.cloned.1.call-start = ((), (), s32[]{:S(2)}) async-start(), calls=%async_computation.8 | async-start | bytes 7864320 | tf_op jit(solution)/shard_map/all_gather | solution.py:108
  63.0 315.4 %reduce-scatter.13.cloned.1.call-start = ((), (), s32[]{:S(2)}) async-start(), calls=%async_computation.11 | async-start | bytes 1769472
  306.9 35.5 %copy-start.10 = (f32[4096,768]{1,0:T(8,128)S(1)}, f32[4096,768]{1,0:T(8,128)}, u32[]{:S(2)}) copy-start(f32[4096,768]{1,0:T(8,128)} %fusion.64) | copy-start | bytes 37748740
  359.0 21.5 %reduce-scatter.11.cloned.1.call-start = ((), (), s32[]{:S(2)}) async-start(), calls=%async_computation.10 | async-start | bytes 1769472 | tf_op jit(solution)/shard_map/reduce_scatter | solution.py:123
  368.8 124.1 %reduce-scatter.9.cloned.1.call-start = ((), (), s32[]{:S(2)}) async-start(), calls=%async_computation.9 | async-start | bytes 7864320 | tf_op jit(solution)/shard_map/reduce_scatter | solution.py:114
  378.3 173.5 %all-reduce.8.cloned.1.call-start = ((), (), s32[]{:S(2)}) async-start(), calls=%async_computation.13 | async-start | bytes 2359296 | tf_op jit(solution)/shard_map/psum | solution.py:131
  380.6 284.5 %reduce-scatter.7.cloned.1.call-start = ((), (), s32[]{:S(2)}) async-start(), calls=%async_computation.7 | async-start | bytes 7864320 | tf_op jit(solution)/shard_map/reduce_scatter | solution.py:101
  389.8 5.9 copy-start.22
  389.9 103.1 %copy-start.20 = (f32[1024]{0:T(1024)S(1)}, f32[1024]{0:T(1024)}, u32[]{:S(2)}) copy-start(f32[1024]{0:T(1024)} %copy-done.19) | copy-start | bytes 12292
  389.9 103.1 %copy-start.24 = (f32[768]{0:T(1024)S(1)}, f32[768]{0:T(1024)}, u32[]{:S(2)}) copy-start(f32[768]{0:T(1024)} %param.21) | copy-start | bytes 9220
  389.9 475.4 %all-reduce.6.cloned.1.call-start = ((), (), s32[]{:S(2)}) async-start(), calls=%async_computation.12 | async-start | bytes 18874368 | tf_op jit(solution)/shard_map/psum | solution.py:181
  397.0 100.0 %copy-start.26 = (f32[1024]{0:T(1024)S(1)}, f32[1024]{0:T(1024)}, u32[]{:S(2)}) copy-start(f32[1024]{0:T(1024)} %copy-done.25) | copy-start | bytes 12292
  493.0 4.1 copy-start.41
  493.0 4.1 copy-start.3
  493.0 4.1 copy-start.8
  497.0 2.8 copy-start.9
  497.1 3.9 copy-start.31
  499.9 7.1 slice-start
  501.1 5.8 slice-start.1
  510.1 3.1 copy-start.18
  520.6 2.9 copy-start.16
  520.6 3.4 copy-start.55
  524.0 2.9 copy-start.13
  524.0 2.9 copy-start.5
  524.0 2.9 copy-start.28
  524.0 2.9 copy-start.36
  524.0 2.9 copy-start.43
  524.0 2.9 copy-start.54
  568.4 3.1 copy-start.39
  568.4 3.1 copy-start.6
  568.4 3.8 copy-start.7
  568.4 3.8 copy-start.37
  568.4 3.8 copy-start.44
  672.2 5.2 copy-start.47
  672.2 5.2 copy-start.48
  672.2 5.2 copy-start.49
  672.2 5.2 copy-start.51
  865.3 6.6 copy-start.14
  (20 other events, 29.7 us)
Sparse Core Ops, SparseCore 0:
  9.6 11.9 all-gather.6
  61.8 118.1 all-gather.4
  181.5 7.3 all-gather.8
  190.3 116.4 all-gather.10
  359.1 6.8 reduce-scatter.12
  369.0 9.6 reduce-scatter.10
  381.0 111.9 reduce-scatter.8
  496.6 55.1 all-reduce.7
  554.3 110.7 reduce-scatter.6
  672.4 192.8 all-reduce.5
where the time goes:
time: 887 us; the launch traced here: 881 us
  waiting for transfers between devices  585 us (66%)
  matrix products  140 us (16%)
  other arithmetic  53.7 us (6%)
  local copies, waits for them, and re-layouts  43.7 us (5%)
  blocking collectives  43.1 us (5%)
  between operations  15.1 us (2%)
    psum x1, waiting for transfers between devices, per_device(): lax.psum((grad_wqkv, grad_wout, grad_gain_one, grad_shift_one, grad_gain_...  145 us
    all_gather x1, waiting for transfers between devices, per_device(): rows_all = lax.all_gather(normed_two_low, 'hid', axis=0, tiled=True)  117 us
    all_gather x1, waiting for transfers between devices, per_device(): cot_all = lax.all_gather(cotangent, 'hid', axis=0, tiled=True)  116 us
    reduce_scatter x1, waiting for transfers between devices, per_device(): lax.psum_scatter(jnp.einsum('tf,df->td', piece, local_in, preferred_eleme...  95.9 us
    reduce_scatter x1, waiting for transfers between devices, per_device(): lax.psum_scatter(jnp.dot(piece, local_back, preferred_element_type=jnp.fl...  90.3 us
    psum x1, blocking collectives, per_device(): lax.psum((grad_wqkv, grad_wout, grad_gain_one, grad_shift_one, grad_gain_...  43.1 us
    dot_general x1, matrix products, per_device(): jnp.einsum('td,fd->tf', cot_all, local_back, preferred_element_type=jnp.f...  35.5 us
    unnamed x124, local copies, waits for them, and re-layouts  32.7 us
  transfers between devices with their start and end apart: 10, of which 6 were waited for; matrix products, arithmetic and copies ran while one was open for 19% of the time, Pallas kernels for 0%

commit v1 on v0

v1 whole, which is shorter than its diff:
```python
import functools

import jax
import jax.numpy as jnp
from jax import lax
from jax.experimental import pallas as pl
from jax.experimental.pallas import tpu as pltpu
from jax.sharding import PartitionSpec as P

H = 12
DH = 64
C = 100
LEN = 1024
LANES = 128
GROUP = 4
WIDE = GROUP * DH

EPSILON = 1e-05
NEGATIVE = -1e30
MIB = 2**20
f32 = jnp.float32
bf16 = jnp.bfloat16

NN = (((1,), (0,)), ((), ()))
NT = (((1,), (1,)), ((), ()))
TN = (((0,), (0,)), ((), ()))
ANY = pl.BlockSpec(memory_space=pl.ANY)


def mm(a, b, dims=NN):
    return lax.dot_general(a, b, dims, preferred_element_type=f32)


def row_stats(x):
    mean = jnp.mean(x, axis=-1, keepdims=True)
    centered = x - mean
    var = jnp.mean(centered * centered, axis=-1, keepdims=True)
    r = lax.rsqrt(var + EPSILON)
    return centered * r, r


def norm_back(g, gain, xhat, r):
    gx = g * gain
    return r * (
        gx
        - jnp.mean(gx, axis=-1, keepdims=True)
        - xhat * jnp.mean(gx * xhat, axis=-1, keepdims=True)
    )


def member_pair(cl, p):
    rows = cl.shape[0]
    lane = lax.broadcasted_iota(jnp.int32, (rows, LANES), 1)
    halves = [(cl[:, 2 * p + i : 2 * p + i + 1] == lane).astype(f32) for i in (0, 1)]
    return jnp.concatenate(halves, axis=1)


def pair_mask():
    d = lax.broadcasted_iota(jnp.int32, (2 * DH, 2 * LANES), 0)
    c = lax.broadcasted_iota(jnp.int32, (2 * DH, 2 * LANES), 1)
    return ((d >= DH) == (c >= LANES)).astype(f32)


def forward_body(
    tok, cl, keep, wq, wk, wv, wo, g1, s1, g2, s2,
    n1, k_out, v_out, mixed, prob, cen, cnt, res, n2,
    acc,
):
    step = pl.program_id(0)
    tile = 256
    rows = tok.shape[0]

    @pl.when(step == 0)
    def _():
        def first_norm(i, _):
            at = pl.ds(pl.multiple_of(i * tile, tile), tile)
            xhat, _r = row_stats(tok[at, :].astype(f32))
            n1[at, :] = (xhat * g1[...] + s1[...]).astype(bf16)
            return 0

        lax.fori_loop(0, rows // tile, first_norm, 0)

    q = mm(n1[...], wq[...]).astype(bf16)
    k = mm(n1[...], wk[...]).astype(bf16)
    v = mm(n1[...], wv[...]).astype(bf16)
    k_out[...] = k
    v_out[...] = v
    same = pair_mask()
    kept = keep[...] == 1
    parts = []
    for p in range(GROUP // 2):
        cols = slice(2 * DH * p, 2 * DH * (p + 1))
        m32 = member_pair(cl[0], p)
        m = m32.astype(bf16)
        count = jnp.maximum(jnp.sum(m32, axis=0, keepdims=True), 1.0)
        centre = (mm(q[:, cols], m, TN) / count * same).astype(bf16)
        score = mm(k[:, cols], centre) * (DH**-0.5)
        score = jnp.where(kept, score, NEGATIVE)
        powered = jnp.exp(score - jnp.max(score, axis=0, keepdims=True))
        pr = (powered * (1.0 / jnp.sum(powered, axis=0, keepdims=True))).astype(bf16)
        centre_out = (mm(v[:, cols], pr, TN) * same).astype(bf16)
        parts.append(mm(m, centre_out, NT).astype(bf16))
        prob[:, 2 * LANES * p : 2 * LANES * (p + 1)] = pr
        cen[p] = centre
        cnt[p] = count
    mix = jnp.concatenate(parts, axis=1)
    mixed[...] = mix
    part = mm(mix, wo[...])

    @pl.when(step == 0)
    def _():
        acc[...] = part

    @pl.when(step > 0)
    def _():
        acc[...] += part

    @pl.when(step == pl.num_programs(0) - 1)
    def _():
        def second_norm(i, _):
            at = pl.ds(pl.multiple_of(i * tile, tile), tile)
            x = tok[at, :].astype(f32) + acc[at, :]
            res[at, :] = x
            xhat, _r = row_stats(x)
            n2[at, :] = (xhat * g2[...] + s2[...]).astype(bf16)
            return 0

        lax.fori_loop(0, rows // tile, second_norm, 0)


def whole(shape):
    return pl.BlockSpec(shape, lambda g: (0,) * len(shape))


def attention_forward(tokens, cl3, keep, wqkv, wo, g1, s1, g2, s2):
    rows, width = tokens.shape
    steps = H // GROUP
    pairs = GROUP // 2
    vec = whole((1, width))
    col = lambda off: pl.BlockSpec((width, WIDE), lambda g: (0, off + g))
    tall = pl.BlockSpec((rows, WIDE), lambda g: (0, g))
    sds = jax.ShapeDtypeStruct
    return pl.pallas_call(
        forward_body,
        grid=(steps,),
        in_specs=[
            whole((rows, width)),
            pl.BlockSpec((1, rows, GROUP), lambda g: (g, 0, 0)),
            whole((rows, 1)),
            col(0), col(steps), col(2 * steps),
            pl.BlockSpec((WIDE, width), lambda g: (g, 0)),
            vec, vec, vec, vec,
        ],
        out_specs=(
            whole((rows, width)),
            tall, tall, tall,
            pl.BlockSpec((rows, GROUP * LANES), lambda g: (0, g)),
            pl.BlockSpec((pairs, 2 * DH, 2 * LANES), lambda g: (g, 0, 0)),
            pl.BlockSpec((pairs, 1, 2 * LANES), lambda g: (g, 0, 0)),
            whole((rows, width)),
            whole((rows, width)),
        ),
        out_shape=(
            sds((rows, width), bf16),
            sds((rows, width), bf16),
            sds((rows, width), bf16),
            sds((rows, width), bf16),
            sds((rows, H * LANES), bf16),
            sds((H // 2, 2 * DH, 2 * LANES), bf16),
            sds((H // 2, 1, 2 * LANES), f32),
            sds((rows, width), f32),
            sds((rows, width), bf16),
        ),
        scratch_shapes=[pltpu.VMEM((rows, width), f32)],
        compiler_params=pltpu.CompilerParams(vmem_limit_bytes=56 * MIB),
        name="attention_forward",
    )(tokens, cl3, keep, wqkv, wqkv, wqkv, wo, g1, s1, g2, s2)


def backward_body(
    gn2, cot, res, tok, n1, k_in, v_in, mixed, prob, cen, cnt, cl, wq, wk, wv, wo, g1, g2,
    gq_w, gk_w, gv_w, go_w, dx, vecs,
    gres, ga, acc,
):
    step = pl.program_id(0)
    tile = 256
    rows, width = tok.shape

    @pl.when(step == 0)
    def _():
        def second_norm(i, carry):
            at = pl.ds(pl.multiple_of(i * tile, tile), tile)
            g = gn2[at, :]
            xhat, r = row_stats(res[at, :])
            out = cot[at, :].astype(f32) + norm_back(g, g2[...], xhat, r)
            gres[at, :] = out
            ga[at, :] = out.astype(bf16)
            return (
                carry[0] + jnp.sum(g * xhat, axis=0, keepdims=True),
                carry[1] + jnp.sum(g, axis=0, keepdims=True),
            )

        zero = jnp.zeros((1, width), f32)
        gain, shift = lax.fori_loop(0, rows // tile, second_norm, (zero, zero))
        vecs[2:3, :] = gain
        vecs[3:4, :] = shift
        vecs[4:8, :] = jnp.zeros((4, width), f32)

    go_w[...] = mm(mixed[...], ga[...], TN).astype(bf16)
    gm = mm(ga[...], wo[...], NT).astype(bf16)
    same = pair_mask()
    gqs, gks, gvs = [], [], []
    for p in range(GROUP // 2):
        cols = slice(2 * DH * p, 2 * DH * (p + 1))
        m = member_pair(cl[0], p).astype(bf16)
        centre = cen[p]
        gco = (mm(gm[:, cols], m, TN) * same).astype(bf16)
        pr = prob[:, 2 * LANES * p : 2 * LANES * (p + 1)]
        gvs.append(mm(pr, gco, NT).astype(bf16))
        pr32 = pr.astype(f32)
        weighted = pr32 * mm(v_in[:, cols], gco)
        gs = (weighted - pr32 * jnp.sum(weighted, axis=0, keepdims=True)).astype(bf16)
        gc = (mm(k_in[:, cols], gs, TN) * (same * DH**-0.5)).astype(bf16)
        gc = (gc.astype(f32) / cnt[p]).astype(bf16)
        gks.append((mm(gs, centre, NT) * (DH**-0.5)).astype(bf16))
        gqs.append(mm(m, gc, NT).astype(bf16))
    gq = jnp.concatenate(gqs, axis=1)
    gk = jnp.concatenate(gks, axis=1)
    gv = jnp.concatenate(gvs, axis=1)
    gq_w[...] = mm(n1[...], gq, TN).astype(bf16)
    gk_w[...] = mm(n1[...], gk, TN).astype(bf16)
    gv_w[...] = mm(n1[...], gv, TN).astype(bf16)
    part = mm(gq, wq[...], NT) + mm(gk, wk[...], NT) + mm(gv, wv[...], NT)

    @pl.when(step == 0)
    def _():
        acc[...] = part

    @pl.when(step > 0)
    def _():
        acc[...] += part

    @pl.when(step == pl.num_programs(0) - 1)
    def _():
        def first_norm(i, carry):
            at = pl.ds(pl.multiple_of(i * tile, tile), tile)
            g = acc[at, :]
            xhat, r = row_stats(tok[at, :].astype(f32))
            dx[at, :] = (gres[at, :] + norm_back(g, g1[...], xhat, r)).astype(bf16)
            return (
                carry[0] + jnp.sum(g * xhat, axis=0, keepdims=True),
                carry[1] + jnp.sum(g, axis=0, keepdims=True),
            )

        zero = jnp.zeros((1, width), f32)
        gain, shift = lax.fori_loop(0, rows // tile, first_norm, (zero, zero))
        vecs[0:1, :] = gain
        vecs[1:2, :] = shift


def attention_backward(gn2, cot, res, tok, n1, k, v, mixed, prob, cen, cnt, cl3, wqkv, wo, g1, g2):
    rows, width = tok.shape
    steps = H // GROUP
    pairs = GROUP // 2
    vec = whole((1, width))
    full = whole((rows, width))
    col = lambda off: pl.BlockSpec((width, WIDE), lambda g: (0, off + g))
    tall = pl.BlockSpec((rows, WIDE), lambda g: (0, g))
    sds = jax.ShapeDtypeStruct
    return pl.pallas_call(
        backward_body,
        grid=(steps,),
        in_specs=[
            full, full, full, full, full,
            tall, tall, tall,
            pl.BlockSpec((rows, GROUP * LANES), lambda g: (0, g)),
            pl.BlockSpec((pairs, 2 * DH, 2 * LANES), lambda g: (g, 0, 0)),
            pl.BlockSpec((pairs, 1, 2 * LANES), lambda g: (g, 0, 0)),
            pl.BlockSpec((1, rows, GROUP), lambda g: (g, 0, 0)),
            col(0), col(steps), col(2 * steps),
            pl.BlockSpec((WIDE, width), lambda g: (g, 0)),
            vec, vec,
        ],
        out_specs=(
            pl.BlockSpec((width, WIDE), lambda g: (0, g)),
            pl.BlockSpec((width, WIDE), lambda g: (0, g)),
            pl.BlockSpec((width, WIDE), lambda g: (0, g)),
            pl.BlockSpec((WIDE, width), lambda g: (g, 0)),
            full,
            whole((8, width)),
        ),
        out_shape=(
            sds((width, width), bf16),
            sds((width, width), bf16),
            sds((width, width), bf16),
            sds((width, width), bf16),
            sds((rows, width), bf16),
            sds((8, width), f32),
        ),
        scratch_shapes=[
            pltpu.VMEM((rows, width), f32),
            pltpu.VMEM((rows, width), bf16),
            pltpu.VMEM((rows, width), f32),
        ],
        compiler_params=pltpu.CompilerParams(vmem_limit_bytes=58 * MIB),
        name="attention_backward",
    )(gn2, cot, res, tok, n1, k, v, mixed, prob, cen, cnt, cl3, wqkv, wqkv, wqkv, wo, g1, g2)


def gelu_parts(x):
    t = 1.0 / (1.0 + (0.3275911 * 0.5**0.5) * jnp.abs(x))
    e = jnp.exp(-0.5 * x * x)
    poly = t * (
        0.254829592
        + t * (-0.284496736 + t * (1.421413741 + t * (-1.453152027 + t * 1.061405429)))
    )
    q = 0.5 * poly * e
    phi = jnp.where(x >= 0, 1.0 - q, q)
    return x * phi, phi + x * e * 0.3989422804014327


def forward_slot(first, places, *refs):
    n_w = len(places)
    n2, cot = refs[:2]
    weights = refs[2 : 2 + n_w]
    i = 2 + n_w
    if not first:
        br_in, gn_in = refs[i : i + 2]
        i += 2
    br, gn, own, other = refs[i : i + 4]
    i += 4
    (n2_s, cot_s, n2t_s, cott_s, up_s, down_s, act_s, gp_s, br_s, gn_s, g_s) = refs[i : i + 11]
    load_sem, weight_sem, acc_sem, out_sem = refs[i + 11 :]
    rows, width = n2_s.shape
    hidden = up_s.shape[1]
    half = width // 2
    tile = 512
    core = lax.axis_index("mod")
    spot = lax.rem(lax.axis_index("dp"), 4)

    acts = [
        pltpu.make_async_copy(n2, n2_s, load_sem.at[0]),
        pltpu.make_async_copy(cot, cot_s, load_sem.at[1]),
    ]
    loads = []
    for at, (ref, (is_up, core_rel, spot_rel)) in enumerate(zip(weights, places)):
        d0 = pl.multiple_of((core ^ core_rel) * half, half)
        if spot_rel is None:
            target = up_s.at[pl.ds(d0, half), :] if is_up else down_s.at[:, pl.ds(d0, half)]
        elif is_up:
            n = half // 4
            target = up_s.at[pl.ds(pl.multiple_of(d0 + (spot ^ spot_rel) * n, n), n), :]
        else:
            n = hidden // 4
            target = down_s.at[
                pl.ds(pl.multiple_of((spot ^ spot_rel) * n, n), n), pl.ds(d0, half)
            ]
        loads.append(pltpu.make_async_copy(ref, target, weight_sem.at[at]))
    for copy in acts + loads:
        copy.start()
    if not first:
        sums = [
            pltpu.make_async_copy(br_in, br_s, acc_sem.at[0]),
            pltpu.make_async_copy(gn_in, gn_s, acc_sem.at[1]),
        ]
        for copy in sums:
            copy.start()
    for copy in acts + loads:
        copy.wait()

    def hidden_rows(i, _):
        at = pl.ds(pl.multiple_of(i * tile, tile), tile)
        h = mm(n2_s[at, :], up_s[...])
        ga = mm(cot_s[at, :], down_s[...], NT)
        act, slope = gelu_parts(h)
        act_s[at, :] = act.astype(bf16)
        gp_s[at, :] = (ga * slope).astype(bf16)
        n2t_s[:, at] = n2_s[at, :].T
        cott_s[:, at] = cot_s[at, :].T
        return 0

    lax.fori_loop(0, rows // tile, hidden_rows, 0)
    dtile = half

    def weight_rows(i, _):
        at = pl.ds(pl.multiple_of(i * dtile, dtile), dtile)
        g_s[0, at, :] = mm(n2t_s[at, :], gp_s[...]).astype(bf16)
        g_s[1, at, :] = mm(cott_s[at, :], act_s[...]).astype(bf16)
        return 0

    lax.fori_loop(0, width // dtile, weight_rows, 0)
    outs = []
    for n, (out, rel) in enumerate(((own, 0), (other, 1))):
        at = pl.ds(pl.multiple_of((core ^ rel) * half, half), half)
        outs.append(pltpu.make_async_copy(g_s.at[:, at, :], out, out_sem.at[n]))
    for copy in outs:
        copy.start()
    if not first:
        for copy in sums:
            copy.wait()

    def token_rows(i, _):
        at = pl.ds(pl.multiple_of(i * tile, tile), tile)
        b = mm(act_s[at, :], down_s[...])
        g = mm(gp_s[at, :], up_s[...], NT)
        if first:
            br_s[at, :] = b
            gn_s[at, :] = g
        else:
            br_s[at, :] += b
            gn_s[at, :] += g
        return 0

    lax.fori_loop(0, rows // tile, token_rows, 0)
    outs.append(pltpu.make_async_copy(br_s, br, out_sem.at[2]))
    outs.append(pltpu.make_async_copy(gn_s, gn, out_sem.at[3]))
    for copy in outs[2:]:
        copy.start()
    for copy in outs:
        copy.wait()


def feed_forward_slot(n2, cot, pieces, sums, hidden):
    rows, width = n2.shape
    half = width // 2
    places = tuple(place for _, place in pieces)
    args = [n2, cot] + [a for a, _ in pieces] + list(sums or ())
    sds = jax.ShapeDtypeStruct
    V = pltpu.VMEM
    D = pltpu.SemaphoreType.DMA
    return pl.pallas_call(
        functools.partial(forward_slot, sums is None, places),
        in_specs=[ANY] * len(args),
        out_specs=(ANY,) * 4,
        out_shape=(
            sds((rows, width), f32),
            sds((rows, width), f32),
            sds((2, half, hidden), bf16),
            sds((2, half, hidden), bf16),
        ),
        scratch_shapes=[
            V((rows, width), bf16),
            V((rows, width), bf16),
            V((width, rows), bf16),
            V((width, rows), bf16),
            V((width, hidden), bf16),
            V((hidden, width), bf16),
            V((rows, hidden), bf16),
            V((rows, hidden), bf16),
            V((rows, width), f32),
            V((rows, width), f32),
            V((2, width, hidden), bf16),
            D((2,)),
            D((len(places),)),
            D((2,)),
            D((4,)),
        ],
        compiler_params=pltpu.CompilerParams(vmem_limit_bytes=56 * MIB),
        name="feed_forward",
    )(*args)


def flip(x, axis, bit):
    n = lax.axis_size(axis)
    return lax.ppermute(x, axis, [(i, i ^ (1 << bit)) for i in range(n)])


def turn(x, axis):
    n = lax.axis_size(axis)
    return lax.ppermute(x, axis, [(i, (i + 1) % n) for i in range(n)])


def take(x, index, n):
    return lax.dynamic_slice_in_dim(x, index * n, n, 0)


def halve(x, axis, bit, mine):
    n = x.shape[0] // 2
    return take(x, mine, n) + flip(take(x, 1 - mine, n), axis, bit)


def join(x, axis, bit, mine):
    y = flip(x, axis, bit)
    return jnp.where(mine == 0, jnp.concatenate([x, y]), jnp.concatenate([y, x]))


def bits(axis):
    return lax.axis_size(axis).bit_length() - 1


def plane_scatter(x, order, spot_bits):
    for b in order:
        x = halve(x, "dp", b, spot_bits[b])
    for b in range(2, bits("dp")):
        x = x + flip(x, "dp", b)
    return x


def plane_gather(x, order, spot_bits):
    for b in reversed(order):
        x = join(x, "dp", b, spot_bits[b])
    return x


def sum_everywhere(x, core, spot_bits):
    x = halve(x, "mod", 0, core)
    n = x.shape[0] // 2
    parts = [plane_scatter(x[:n], (0, 1), spot_bits), plane_scatter(x[n:], (1, 0), spot_bits)]
    x = jnp.concatenate(parts)
    for b in range(bits("hid")):
        x = x + flip(x, "hid", b)
    n = x.shape[0] // 2
    parts = [plane_gather(x[:n], (0, 1), spot_bits), plane_gather(x[n:], (1, 0), spot_bits)]
    return join(jnp.concatenate(parts), "mod", 0, core)


def per_device(
    tokens, clusters, key_mask, query_key_value_weight, attention_output_weight, up_weight,
    down_weight, gain_one, shift_one, gain_two, shift_two, cotangent,
):
    rows, width = tokens.shape
    half = width // 2
    hidden = up_weight.shape[1]
    ring = lax.axis_size("hid")
    core = lax.axis_index("mod")
    spot = lax.rem(lax.axis_index("dp"), 4)
    spot_bits = (spot & 1, spot >> 1)

    slots = [
        [
            (up_weight, (True, 0, None)),
            (down_weight, (False, 0, None)),
            (flip(up_weight, "mod", 0), (True, 1, None)),
            (flip(down_weight, "mod", 0), (False, 1, None)),
        ]
    ]
    a = take(up_weight, spot, half // 4)
    b = take(down_weight, spot, hidden // 4)
    for _ in range(1, ring):
        a, b = turn(a, "hid"), turn(b, "hid")
        ax, by = flip(a, "dp", 0), flip(b, "dp", 1)
        held = [
            (a, (True, 0, 0)),
            (ax, (True, 0, 1)),
            (flip(a, "dp", 1), (True, 0, 2)),
            (flip(ax, "dp", 1), (True, 0, 3)),
            (b, (False, 0, 0)),
            (by, (False, 0, 2)),
            (flip(b, "dp", 0), (False, 0, 1)),
            (flip(by, "dp", 0), (False, 0, 3)),
        ]
        held += [(flip(x, "mod", 0), (is_up, 1, s)) for x, (is_up, _, s) in held]
        slots.append(held)

    cl3 = clusters.reshape(rows, H // GROUP, GROUP).transpose(1, 0, 2)
    keep = key_mask.reshape(rows, 1)
    vec = lambda x: x.reshape(1, width)
    g1, s1, g2, s2 = vec(gain_one), vec(shift_one), vec(gain_two), vec(shift_two)
    n1, k, v, mixed, prob, cen, cnt, res, n2 = attention_forward(
        tokens, cl3, keep, query_key_value_weight, attention_output_weight, g1, s1, g2, s2
    )

    sums = None
    shares = []
    for pieces in slots:
        *sums, own, other = feed_forward_slot(n2, cotangent, pieces, sums, hidden)
        part = own + flip(other, "mod", 0)
        shares.append(
            jnp.stack(
                [
                    plane_scatter(part[0], (0, 1), spot_bits),
                    plane_scatter(part[1], (1, 0), spot_bits),
                ]
            )
        )
    branch, gn2 = sums
    output = (res + branch).astype(bf16)

    total = shares[1 % ring]
    for s in range(2, ring + 1):
        total = turn(total, "hid") + shares[s % ring]
    grad_in = plane_gather(total[0], (0, 1), spot_bits).astype(f32)
    grad_back = plane_gather(total[1], (1, 0), spot_bits).T.astype(f32)

    gq, gk, gv, go, input_grad, vecs = attention_backward(
        gn2, cotangent, res, tokens, n1, k, v, mixed, prob, cen, cnt, cl3,
        query_key_value_weight, attention_output_weight, g1, g2,
    )
    for axis in ("mod", "dp", "hid"):
        for bit in range(bits(axis)):
            vecs = vecs + flip(vecs, axis, bit)
    gqkv = jnp.concatenate([sum_everywhere(x, core, spot_bits) for x in (gq, gk, gv)], axis=1)
    grad_out = sum_everywhere(go, core, spot_bits)
    return (
        output,
        input_grad,
        gqkv.astype(f32),
        grad_out.astype(f32),
        grad_in,
        grad_back,
        vecs[0],
        vecs[1],
        vecs[2],
        vecs[3],
    )


def solution(mesh):
    every = P(("dp", "hid", "mod"), None)
    placed = (
        every, every, P(("dp", "hid", "mod")), P(), P(), P("mod", "hid"), P("hid", "mod"),
        P(), P(), P(), P(), every,
    )
    return jax.shard_map(
        per_device,
        mesh=mesh,
        in_specs=placed,
        out_specs=(every, every, P(), P(), P("mod", "hid"), P("hid", "mod"), P(), P(), P(), P()),
        check_vma=False,
    )
```

time: 887 us -> 451 us (0.51)
  waiting for transfers between devices: 585 us -> 207 us
  matrix products: 140 us -> 0 us
  Pallas kernels: 0 us -> 123 us
  starting transfers between devices: 0.4 us -> 83.2 us
  blocking collectives: 43.1 us -> 0 us
  other arithmetic: 53.7 us -> 16.9 us
  local copies, waits for them, and re-layouts: 43.7 us -> 14.1 us
  between operations: 15.1 us -> 2.41 us
    all_gather x4 -> x0, waiting for transfers between devices: 233 us -> none  [the longest x1 117 us: per_device(): rows_all = lax.all_gather(normed_two_low, 'hid', axis=0, tiled=True)]
    ppermute x0 -> x130, waiting for transfers between devices: none -> 207 us  [the longest x121 173 us: flip(): return lax.ppermute(x, axis, [(i, i ^ 1 << bit) for i in range(n)])]
    reduce_scatter x3 -> x0, waiting for transfers between devices: 186 us -> none  [the longest x1 95.9 us: per_device(): lax.psum_scatter(jnp.einsum('tf,df->td', piece, local_in, preferred_eleme...]
    psum x2 -> x0, waiting for transfers between devices: 163 us -> none  [the longest x1 145 us: per_device(): lax.psum((grad_wqkv, grad_wout, grad_gain_one, grad_shift_one, grad_gain_...]
    dot_general x21 -> x0, matrix products: 140 us -> none  [the longest x1 35.5 us: per_device(): jnp.einsum('td,fd->tf', cot_all, local_back, preferred_element_type=jnp.f...]
    pallas_call x0 -> x6, Pallas kernels: none -> 123 us  [the longest x4 62.6 us: feed_forward_slot(): pl.pallas_call(functools.partial(forward_slot, sums is None, places), in_...]
    ppermute x0 -> x130, starting transfers between devices: none -> 83.2 us  [the longest x121 75.9 us: flip(): return lax.ppermute(x, axis, [(i, i ^ 1 << bit) for i in range(n)])]
    psum x1 -> x0, blocking collectives: 43.1 us -> none  [per_device(): lax.psum((grad_wqkv, grad_wout, grad_gain_one, grad_shift_one, grad_gain_...]
  transfers between devices with their start and end apart: 10 -> 130, of which waited for: 6 -> 75; matrix products, arithmetic and copies ran while one was open for 19% -> 6% of each run, Pallas kernels for 0% -> 28%
where the time goes in v1:
time: 451 us; the launch traced here: 446 us
  waiting for transfers between devices  207 us (46%)
  Pallas kernels  123 us (27%)
  starting transfers between devices  83.2 us (18%)
  other arithmetic  16.9 us (4%)
  local copies, waits for them, and re-layouts  14.1 us (3%)
    ppermute x121, waiting for transfers between devices, flip(): return lax.ppermute(x, axis, [(i, i ^ 1 << bit) for i in range(n)])  173 us
    ppermute x121, starting transfers between devices, flip(): return lax.ppermute(x, axis, [(i, i ^ 1 << bit) for i in range(n)])  75.9 us
    pallas_call x4, Pallas kernels, feed_forward_slot(): pl.pallas_call(functools.partial(forward_slot, sums is None, places), in_...  62.6 us
    pallas_call x1, Pallas kernels, attention_backward(): pl.pallas_call(backward_body, grid=(steps,), in_specs=[full, full, full,...  37.3 us
    ppermute x9, waiting for transfers between devices, turn(): return lax.ppermute(x, axis, [(i, (i + 1) % n) for i in range(n)])  34.1 us
    pallas_call x1, Pallas kernels, attention_forward(): pl.pallas_call(forward_body, grid=(steps,), in_specs=[whole((rows, width)...  22.7 us
  transfers between devices with their start and end apart: 130, of which 75 were waited for; matrix products, arithmetic and copies ran while one was open for 6% of the time, Pallas kernels for 28%

profile of v1, /device:TPU:0, one launch (start us, length us, event | category | flops | bytes accessed | tf_op | source)
XLA Modules:
  0.0 445.9 jit_solution(13634238264685754300)
XLA Ops:
  1.6 3.1 collective-permute-start
  7.3 4.1 collective-permute-done.refs_2_
  17.8 2.6 collective-permute-done.37.refs_7_
  24.9 2.9 collective-permute-done.1.refs_2_
  43.0 6.4 %collective-permute-done.2.refs_2_ = bf16[96,768]{1,0:T(8,128)(2,1)S(1)} collective-permute-done((bf16[96,768]{1,0:T(8,128)(2,1)S(1)}, bf16[96,768]{1,0:T(8,128)(2,1)S(1)}, u32[]{:S(2)}, u32[]{:S(2)}) %collective-permute-start.2) | collective-permute-done | bytes 147488 | tf_op jit(solution)/shard_map/ppermute | solution.py:470
  49.4 2.6 collective-permute-done.8.refs_6_
  54.7 2.6 collective-permute-done.22.refs_5_
  62.9 2.4 collective-permute-done.3.refs_3_
  71.2 2.4 collective-permute-done.5.refs_5_
  82.3 22.7 %attention_forward.1 = (bf16[1024,768]{1,0:T(8,128)(2,1)}, bf16[1024,768]{1,0:T(8,128)(2,1)}, bf16[1024,768]{1,0:T(8,128)(2,1)}, bf16[1024,768]{1,0:T(8,128)(2,1...) custom-call(bf16[1024,768]{1,0:T(8,128)(2,1)} %tok.3, ...), custom_call_target="tpu_custom_call" | custom-call | tf_op jit(solution)/shard_map/attention_forward/pallas_call | solution.py:143
  105.1 14.8 %feed_forward.4 = (f32[1024,768]{1,0:T(8,128)}, f32[1024,768]{1,0:T(8,128)}, bf16[2,384,768]{2,1,0:T(8,128)(2,1)}, bf16[2,384,768]{2,1,0:T(8,128)(2,1)}) custom-call(bf16[1024,768]{1,0:T(8,128)(2,1)} %get-tuple-element.42.refs_0_, bf16[1024,768]{1,0:T(8,128)(2,1)} %cot.1, bf16[384,768]{1,0:T(8,128)(2,1)} %refs_2_.1, bf16[768,384]{1,0:T(8,128)(2,1)} %refs_3_.1, ...), custom_call_target="tpu_custom_call" | custom-call | tf_op jit(solution)/shard_map/feed_forward/pallas_call | solution.py:431
  119.9 16.1 %feed_forward.5 = (f32[1024,768]{1,0:T(8,128)}, f32[1024,768]{1,0:T(8,128)}, bf16[2,384,768]{2,1,0:T(8,128)(2,1)}, bf16[2,384,768]{2,1,0:T(8,128)(2,1)}) custom-call(bf16[1024,768]{1,0:T(8,128)(2,1)} %get-tuple-element.42.refs_0_, bf16[1024,768]{1,0:T(8,128)(2,1)} %cot.1, bf16[96,768]{1,0:T(8,128)(2,1)} %copy-done.11, bf16[96,768]{1,0:T(8,128)(2,1)} %copy-done.13, ...), custom_call_target="tpu_custom_call" | custom-call | tf_op jit(solution)/shard_map/feed_forward/pallas_call | solution.py:431
  136.0 15.9 %feed_forward.6 = (f32[1024,768]{1,0:T(8,128)}, f32[1024,768]{1,0:T(8,128)}, bf16[2,384,768]{2,1,0:T(8,128)(2,1)}, bf16[2,384,768]{2,1,0:T(8,128)(2,1)}) custom-call(bf16[1024,768]{1,0:T(8,128)(2,1)} %get-tuple-element.42.refs_0_, bf16[1024,768]{1,0:T(8,128)(2,1)} %cot.1, bf16[96,768]{1,0:T(8,128)(2,1)} %copy-done.17, bf16[96,768]{1,0:T(8,128)(2,1)} %copy-done.26, ...), custom_call_target="tpu_custom_call" | custom-call | tf_op jit(solution)/shard_map/feed_forward/pallas_call | solution.py:431
  152.6 15.8 %feed_forward.7 = (f32[1024,768]{1,0:T(8,128)}, f32[1024,768]{1,0:T(8,128)}, bf16[2,384,768]{2,1,0:T(8,128)(2,1)}, bf16[2,384,768]{2,1,0:T(8,128)(2,1)}) custom-call(bf16[1024,768]{1,0:T(8,128)(2,1)} %get-tuple-element.42.refs_0_, bf16[1024,768]{1,0:T(8,128)(2,1)} %cot.1, bf16[96,768]{1,0:T(8,128)(2,1)} %copy-done.28, bf16[96,768]{1,0:T(8,128)(2,1)} %copy-done.34, ...), custom_call_target="tpu_custom_call" | custom-call | tf_op jit(solution)/shard_map/feed_forward/pallas_call | solution.py:431
  168.4 37.3 %attention_backward.1 = (bf16[768,768]{1,0:T(8,128)(2,1)}, bf16[768,768]{1,0:T(8,128)(2,1)}, bf16[768,768]{1,0:T(8,128)(2,1)}, bf16[768,768]{1,0:T(8,128)(2,1)},...) custom-call(f32[1024,768]{1,0:T(8,128)} %get-tuple-element.50.gn2, bf16[1024,768]{1,0:T(8,128)(2,1)} %cot.1, ...), custom_call_target="tpu_custom_call" | custom-call | tf_op jit(solution)/shard_map/attention_backward/pallas_call | solution.py:270
  209.3 3.5 add_convert_fusion
  213.3 3.4 collective-permute-done.127
  216.7 3.7 collective-permute-done.128
  220.6 4.7 %collective-permute-done.129 = f32[8,768]{1,0:T(8,128)S(1)} collective-permute-done((f32[8,768]{1,0:T(8,128)S(1)}, f32[8,768]{1,0:T(8,128)S(1)}, u32[]{:S(2)}, u32[]{:S(2)}) %collective-permute-start.129) | collective-permute-done | bytes 24608 | tf_op jit(solution)/shard_map/ppermute | solution.py:465
  232.3 5.5 %collective-permute-done.87 = bf16[96,768]{1,0:T(8,128)(2,1)S(1)} collective-permute-done((bf16[96,768]{1,0:T(8,128)(2,1)S(1)}, bf16[96,768]{1,0:T(8,128)(2,1)S(1)}, u32[]{:S(2)}, u32[]{:S(2)}) %collective-permute-start.87) | collective-permute-done | bytes 147488 | tf_op jit(solution)/shard_map/ppermute | solution.py:465
  238.2 4.9 %collective-permute-done.51 = bf16[96,768]{1,0:T(8,128)(2,1)S(1)} collective-permute-done((bf16[96,768]{1,0:T(8,128)(2,1)S(1)}, bf16[96,768]{1,0:T(8,128)(2,1)S(1)}, u32[]{:S(2)}, u32[]{:S(2)}) %collective-permute-start.51) | collective-permute-done | bytes 147488 | tf_op jit(solution)/shard_map/ppermute | solution.py:465
  243.5 4.7 %collective-permute-done.89 = bf16[96,768]{1,0:T(8,128)(2,1)S(1)} collective-permute-done((bf16[96,768]{1,0:T(8,128)(2,1)S(1)}, bf16[96,768]{1,0:T(8,128)(2,1)S(1)}, u32[]{:S(2)}, u32[]{:S(2)}) %collective-permute-start.89) | collective-permute-done | bytes 147488 | tf_op jit(solution)/shard_map/ppermute | solution.py:465
  248.7 4.7 %collective-permute-done.53 = bf16[96,768]{1,0:T(8,128)(2,1)S(1)} collective-permute-done((bf16[96,768]{1,0:T(8,128)(2,1)S(1)}, bf16[96,768]{1,0:T(8,128)(2,1)S(1)}, u32[]{:S(2)}, u32[]{:S(2)}) %collective-permute-start.53) | collective-permute-done | bytes 147488 | tf_op jit(solution)/shard_map/ppermute | solution.py:465
  253.7 4.8 %collective-permute-done.63 = bf16[96,768]{1,0:T(8,128)(2,1)S(1)} collective-permute-done((bf16[96,768]{1,0:T(8,128)(2,1)S(1)}, bf16[96,768]{1,0:T(8,128)(2,1)S(1)}, u32[]{:S(2)}, u32[]{:S(2)}) %collective-permute-start.63) | collective-permute-done | bytes 147488 | tf_op jit(solution)/shard_map/ppermute | solution.py:465
  259.0 4.6 %collective-permute-done.65 = bf16[96,768]{1,0:T(8,128)(2,1)S(1)} collective-permute-done((bf16[96,768]{1,0:T(8,128)(2,1)S(1)}, bf16[96,768]{1,0:T(8,128)(2,1)S(1)}, u32[]{:S(2)}, u32[]{:S(2)}) %collective-permute-start.65) | collective-permute-done | bytes 147488 | tf_op jit(solution)/shard_map/ppermute | solution.py:465
  264.0 4.7 %collective-permute-done.75 = bf16[96,768]{1,0:T(8,128)(2,1)S(1)} collective-permute-done((bf16[96,768]{1,0:T(8,128)(2,1)S(1)}, bf16[96,768]{1,0:T(8,128)(2,1)S(1)}, u32[]{:S(2)}, u32[]{:S(2)}) %collective-permute-start.75) | collective-permute-done | bytes 147488 | tf_op jit(solution)/shard_map/ppermute | solution.py:465
  269.3 5.1 %collective-permute-done.77 = bf16[96,768]{1,0:T(8,128)(2,1)S(1)} collective-permute-done((bf16[96,768]{1,0:T(8,128)(2,1)S(1)}, bf16[96,768]{1,0:T(8,128)(2,1)S(1)}, u32[]{:S(2)}, u32[]{:S(2)}) %collective-permute-start.77) | collective-permute-done | bytes 147488 | tf_op jit(solution)/shard_map/ppermute | solution.py:465
  274.9 3.9 collective-permute-done.88
  279.2 4.6 %collective-permute-done.52 = bf16[48,768]{1,0:T(8,128)(2,1)S(1)} collective-permute-done((bf16[48,768]{1,0:T(8,128)(2,1)S(1)}, bf16[48,768]{1,0:T(8,128)(2,1)S(1)}, u32[]{:S(2)}, u32[]{:S(2)}) %collective-permute-start.52) | collective-permute-done | bytes 73760 | tf_op jit(solution)/shard_map/ppermute | solution.py:465
  284.1 4.0 collective-permute-done.90
  288.4 4.0 collective-permute-done.54
  292.9 3.9 collective-permute-done.64
  297.1 4.0 collective-permute-done.66
  301.6 4.7 %collective-permute-done.76 = bf16[48,768]{1,0:T(8,128)(2,1)S(1)} collective-permute-done((bf16[48,768]{1,0:T(8,128)(2,1)S(1)}, bf16[48,768]{1,0:T(8,128)(2,1)S(1)}, u32[]{:S(2)}, u32[]{:S(2)}) %collective-permute-start.76) | collective-permute-done | bytes 73760 | tf_op jit(solution)/shard_map/ppermute | solution.py:465
  306.6 4.0 collective-permute-done.78
  324.5 6.1 %collective-permute-done.92 = bf16[96,768]{1,0:T(8,128)(2,1)S(1)} collective-permute-done((bf16[96,768]{1,0:T(8,128)(2,1)S(1)}, bf16[96,768]{1,0:T(8,128)(2,1)S(1)}, u32[]{:S(2)}, u32[]{:S(2)}) %collective-permute-start.92) | collective-permute-done | bytes 147488 | tf_op jit(solution)/shard_map/ppermute | solution.py:465
  330.7 6.0 %collective-permute-done.56 = bf16[96,768]{1,0:T(8,128)(2,1)S(1)} collective-permute-done((bf16[96,768]{1,0:T(8,128)(2,1)S(1)}, bf16[96,768]{1,0:T(8,128)(2,1)S(1)}, u32[]{:S(2)}, u32[]{:S(2)}) %collective-permute-start.56) | collective-permute-done | bytes 147488 | tf_op jit(solution)/shard_map/ppermute | solution.py:465
  336.8 7.0 %collective-permute-done.68 = bf16[96,768]{1,0:T(8,128)(2,1)S(1)} collective-permute-done((bf16[96,768]{1,0:T(8,128)(2,1)S(1)}, bf16[96,768]{1,0:T(8,128)(2,1)S(1)}, u32[]{:S(2)}, u32[]{:S(2)}) %collective-permute-start.68) | collective-permute-done | bytes 147488 | tf_op jit(solution)/shard_map/ppermute | solution.py:465
  343.9 6.1 %collective-permute-done.80 = bf16[96,768]{1,0:T(8,128)(2,1)S(1)} collective-permute-done((bf16[96,768]{1,0:T(8,128)(2,1)S(1)}, bf16[96,768]{1,0:T(8,128)(2,1)S(1)}, u32[]{:S(2)}, u32[]{:S(2)}) %collective-permute-start.80) | collective-permute-done | bytes 147488 | tf_op jit(solution)/shard_map/ppermute | solution.py:465
  354.7 5.2 %collective-permute-done.101 = bf16[192,768]{1,0:T(8,128)(2,1)S(1)} collective-permute-done((bf16[192,768]{1,0:T(8,128)(2,1)S(1)}, bf16[192,768]{1,0:T(8,128)(2,1)S(1)}, u32[]{:S(2)}, u32[]{:S(2)}) %collective-permute-start.101) | collective-permute-done | bytes 294944 | tf_op jit(solution)/shard_map/ppermute | solution.py:465
  362.6 4.5 %collective-permute-done.93 = bf16[48,768]{1,0:T(8,128)(2,1)S(1)} collective-permute-done((bf16[48,768]{1,0:T(8,128)(2,1)S(1)}, bf16[48,768]{1,0:T(8,128)(2,1)S(1)}, u32[]{:S(2)}, u32[]{:S(2)}) %collective-permute-start.93) | collective-permute-done | bytes 73760 | tf_op jit(solution)/shard_map/ppermute | solution.py:465
  406.1 3.7 collective-permute-done.103
  411.0 4.0 collective-permute-done.114
  415.0 4.4 collective-permute-done.109
  420.5 7.6 %collective-permute-done.115 = bf16[2,96,768]{2,1,0:T(8,128)(2,1)S(1)} collective-permute-done((bf16[2,96,768]{2,1,0:T(8,128)(2,1)S(1)}, bf16[2,96,768]{2,1,0:T(8,128)(2,1)S(1)}, u32[]{:S(2)}, u32[]{:S(2)}) %collective-permute-start.115) | collective-permute-done | bytes 294944 | tf_op jit(solution)/shard_map/ppermute | solution.py:470
  430.8 2.5 collective-permute-done.123
  434.5 3.2 maximum_convert_fusion
  442.0 2.6 collective-permute-done.122
  (479 shorter events, 141.6 us)
Async XLA Ops:
  1.6 9.8 %collective-permute-start = (bf16[96,768]{1,0:T(8,128)(2,1)S(1)}, bf16[96,768]{1,0:T(8,128)(2,1)S(1)}, u32[]{:S(2)}, u32[]{:S(2)}) collective-permute-start(bf16[96,768]{1,0:T(8,128)(2,1)S(1)} %constant_dynamic-slice_fusion.29), channel_id=1, source_target_pairs={{0,2},{2,4},{4,6},{6,0},{1,3},{3,5},{5,7},{7,1},{8,10},{10,12},{12... | collective-permute-start | bytes 442376 | tf_op jit(solution)/shard_map/ppermute | solution.py:470
  5.6 8.1 %collective-permute-start.6 = (bf16[192,384]{1,0:T(8,128)(2,1)S(1)}, bf16[192,384]{1,0:T(8,128)(2,1)S(1)}, u32[]{:S(2)}, u32[]{:S(2)}) collective-permute-start(bf16[192,384]{1,0:T(8,128)(2,1)S(1)} %constant_dynamic-slice_fusion.28), channel_id=1, source_target_pairs={{0,2},{2,4},{4,6},{6,0},{1,3},{3,5},{5,7},{7,1},{8,10},{10,12},{12... | collective-permute-start | bytes 442376 | tf_op jit(solution)/shard_map/ppermute | solution.py:470
  17.3 7.7 %collective-permute-start.44 = (bf16[192,384]{1,0:T(8,128)(2,1)S(1)}, bf16[192,384]{1,0:T(8,128)(2,1)S(1)}, u32[]{:S(2)}, u32[]{:S(2)}) collective-permute-start(bf16[192,384]{1,0:T(8,128)(2,1)S(1)} %collective-permute-done.6.refs_6_), channel_id=1, source_target_pairs={{0,1},{1,0},{2,3},{3,2},{4,5},{5,4},{6,7},{7,6},{8,9},{9,8},{10,11... | collective-permute-start | bytes 442376 | tf_op jit(solution)/shard_map/ppermute | solution.py:465
  20.4 7.5 %collective-permute-start.1 = (bf16[96,768]{1,0:T(8,128)(2,1)S(1)}, bf16[96,768]{1,0:T(8,128)(2,1)S(1)}, u32[]{:S(2)}, u32[]{:S(2)}) collective-permute-start(bf16[96,768]{1,0:T(8,128)(2,1)S(1)} %collective-permute-done.refs_2_), channel_id=1, source_target_pairs={{0,2},{2,4},{4,6},{6,0},{1,3},{3,5},{5,7},{7,1},{8,10},{10,12},{12... | collective-permute-start | bytes 442376 | tf_op jit(solution)/shard_map/ppermute | solution.py:470
  21.9 7.5 %collective-permute-start.7 = (bf16[192,384]{1,0:T(8,128)(2,1)S(1)}, bf16[192,384]{1,0:T(8,128)(2,1)S(1)}, u32[]{:S(2)}, u32[]{:S(2)}) collective-permute-start(bf16[192,384]{1,0:T(8,128)(2,1)S(1)} %collective-permute-done.6.refs_6_), channel_id=1, source_target_pairs={{0,2},{2,4},{4,6},{6,0},{1,3},{3,5},{5,7},{7,1},{8,10},{10,12},{12... | collective-permute-start | bytes 442376 | tf_op jit(solution)/shard_map/ppermute | solution.py:470
  22.0 7.5 %collective-permute-start.36 = (bf16[96,768]{1,0:T(8,128)(2,1)S(1)}, bf16[96,768]{1,0:T(8,128)(2,1)S(1)}, u32[]{:S(2)}, u32[]{:S(2)}) collective-permute-start(bf16[96,768]{1,0:T(8,128)(2,1)S(1)} %collective-permute-done.34.refs_3_), channel_id=1, source_target_pairs={{0,16},{8,24},{16,0},{24,8},{1,17},{9,25},{17,1},{25,9},{2,18},{10... | collective-permute-start | bytes 442376 | tf_op jit(solution)/shard_map/ppermute | solution.py:465
  31.2 22.8 %collective-permute-start.48 = (bf16[384,768]{1,0:T(8,128)(2,1)}, bf16[384,768]{1,0:T(8,128)(2,1)S(1)}, u32[]{:S(2)}, u32[]{:S(2)}) collective-permute-start(bf16[384,768]{1,0:T(8,128)(2,1)} %refs_2_.1), channel_id=1, source_target_pairs={{0,1},{1,0},{2,3},{3,2},{4,5},{5,4},{6,7},{7,6},{8,9},{9,8},{10,11... | collective-permute-start | bytes 1769480 | tf_op jit(solution)/shard_map/ppermute | solution.py:465
  31.3 23.3 %collective-permute-start.49 = (bf16[768,384]{1,0:T(8,128)(2,1)}, bf16[768,384]{1,0:T(8,128)(2,1)S(1)}, u32[]{:S(2)}, u32[]{:S(2)}) collective-permute-start(bf16[768,384]{1,0:T(8,128)(2,1)} %refs_3_.1), channel_id=1, source_target_pairs={{0,1},{1,0},{2,3},{3,2},{4,5},{5,4},{6,7},{7,6},{8,9},{9,8},{10,11... | collective-permute-start | bytes 1769480 | tf_op jit(solution)/shard_map/ppermute | solution.py:465
  31.8 6.7 %collective-permute-start.23 = (bf16[192,384]{1,0:T(8,128)(2,1)S(1)}, bf16[192,384]{1,0:T(8,128)(2,1)S(1)}, u32[]{:S(2)}, u32[]{:S(2)}) collective-permute-start(bf16[192,384]{1,0:T(8,128)(2,1)S(1)} %collective-permute-done.7.refs_6_), channel_id=1, source_target_pairs={{0,16},{8,24},{16,0},{24,8},{1,17},{9,25},{17,1},{25,9},{2,18},{10... | collective-permute-start | bytes 442376 | tf_op jit(solution)/shard_map/ppermute | solution.py:465
  33.3 7.5 %collective-permute-start.21 = (bf16[96,768]{1,0:T(8,128)(2,1)S(1)}, bf16[96,768]{1,0:T(8,128)(2,1)S(1)}, u32[]{:S(2)}, u32[]{:S(2)}) collective-permute-start(bf16[96,768]{1,0:T(8,128)(2,1)S(1)} %collective-permute-done.1.refs_2_), channel_id=1, source_target_pairs={{0,16},{8,24},{16,0},{24,8},{1,17},{9,25},{17,1},{25,9},{2,18},{10... | collective-permute-start | bytes 442376 | tf_op jit(solution)/shard_map/ppermute | solution.py:465
  40.9 8.5 %collective-permute-start.2 = (bf16[96,768]{1,0:T(8,128)(2,1)S(1)}, bf16[96,768]{1,0:T(8,128)(2,1)S(1)}, u32[]{:S(2)}, u32[]{:S(2)}) collective-permute-start(bf16[96,768]{1,0:T(8,128)(2,1)S(1)} %collective-permute-done.1.refs_2_), channel_id=1, source_target_pairs={{0,2},{2,4},{4,6},{6,0},{1,3},{3,5},{5,7},{7,1},{8,10},{10,12},{12... | collective-permute-start | bytes 442376 | tf_op jit(solution)/shard_map/ppermute | solution.py:470
  41.0 11.0 %collective-permute-start.8 = (bf16[192,384]{1,0:T(8,128)(2,1)S(1)}, bf16[192,384]{1,0:T(8,128)(2,1)S(1)}, u32[]{:S(2)}, u32[]{:S(2)}) collective-permute-start(bf16[192,384]{1,0:T(8,128)(2,1)S(1)} %collective-permute-done.7.refs_6_), channel_id=1, source_target_pairs={{0,2},{2,4},{4,6},{6,0},{1,3},{3,5},{5,7},{7,1},{8,10},{10,12},{12... | collective-permute-start | bytes 442376 | tf_op jit(solution)/shard_map/ppermute | solution.py:470
  43.0 10.5 %collective-permute-start.43 = (bf16[96,768]{1,0:T(8,128)(2,1)S(1)}, bf16[96,768]{1,0:T(8,128)(2,1)S(1)}, u32[]{:S(2)}, u32[]{:S(2)}) collective-permute-start(bf16[96,768]{1,0:T(8,128)(2,1)S(1)} %collective-permute-done.36.refs_5_), channel_id=1, source_target_pairs={{0,1},{1,0},{2,3},{3,2},{4,5},{5,4},{6,7},{7,6},{8,9},{9,8},{10,11... | collective-permute-start | bytes 442376 | tf_op jit(solution)/shard_map/ppermute | solution.py:465
  54.6 6.7 %collective-permute-start.28 = (bf16[96,768]{1,0:T(8,128)(2,1)S(1)}, bf16[96,768]{1,0:T(8,128)(2,1)S(1)}, u32[]{:S(2)}, u32[]{:S(2)}) collective-permute-start(bf16[96,768]{1,0:T(8,128)(2,1)S(1)} %collective-permute-done.21.refs_4_), channel_id=1, source_target_pairs={{0,1},{1,0},{2,3},{3,2},{4,5},{5,4},{6,7},{7,6},{8,9},{9,8},{10,11... | collective-permute-start | bytes 442376 | tf_op jit(solution)/shard_map/ppermute | solution.py:465
  60.0 7.3 %collective-permute-start.4 = (bf16[96,768]{1,0:T(8,128)(2,1)S(1)}, bf16[96,768]{1,0:T(8,128)(2,1)}, u32[]{:S(2)}, u32[]{:S(2)}) collective-permute-start(bf16[96,768]{1,0:T(8,128)(2,1)S(1)} %collective-permute-done.2.refs_2_), channel_id=1, source_target_pairs={{0,16},{8,24},{16,0},{24,8},{1,17},{9,25},{17,1},{25,9},{2,18},{10... | collective-permute-start | bytes 442376 | tf_op jit(solution)/shard_map/ppermute | solution.py:465
  70.6 81.3 %collective-permute-start.17 = (bf16[192,384]{1,0:T(8,128)(2,1)}, bf16[192,384]{1,0:T(8,128)(2,1)}, u32[]{:S(2)}, u32[]{:S(2)}) collective-permute-start(bf16[192,384]{1,0:T(8,128)(2,1)} %collective-permute-done.9.refs_7_), channel_id=1, source_target_pairs={{0,1},{1,0},{2,3},{3,2},{4,5},{5,4},{6,7},{7,6},{8,9},{9,8},{10,11... | collective-permute-start | bytes 442376 | tf_op jit(solution)/shard_map/ppermute | solution.py:465
  71.1 80.9 %collective-permute-start.14 = (bf16[96,768]{1,0:T(8,128)(2,1)}, bf16[96,768]{1,0:T(8,128)(2,1)}, u32[]{:S(2)}, u32[]{:S(2)}) collective-permute-start(bf16[96,768]{1,0:T(8,128)(2,1)} %collective-permute-done.4.refs_4_), channel_id=1, source_target_pairs={{0,1},{1,0},{2,3},{3,2},{4,5},{5,4},{6,7},{7,6},{8,9},{9,8},{10,11... | collective-permute-start | bytes 442376 | tf_op jit(solution)/shard_map/ppermute | solution.py:465
  73.6 78.8 %collective-permute-start.18 = (bf16[192,384]{1,0:T(8,128)(2,1)}, bf16[192,384]{1,0:T(8,128)(2,1)}, u32[]{:S(2)}, u32[]{:S(2)}) collective-permute-start(bf16[192,384]{1,0:T(8,128)(2,1)} %collective-permute-done.10.refs_8_), channel_id=1, source_target_pairs={{0,1},{1,0},{2,3},{3,2},{4,5},{5,4},{6,7},{7,6},{8,9},{9,8},{10,11... | collective-permute-start | bytes 442376 | tf_op jit(solution)/shard_map/ppermute | solution.py:465
  75.0 77.5 %collective-permute-start.15 = (bf16[96,768]{1,0:T(8,128)(2,1)}, bf16[96,768]{1,0:T(8,128)(2,1)}, u32[]{:S(2)}, u32[]{:S(2)}) collective-permute-start(bf16[96,768]{1,0:T(8,128)(2,1)} %collective-permute-done.5.refs_5_), channel_id=1, source_target_pairs={{0,1},{1,0},{2,3},{3,2},{4,5},{5,4},{6,7},{7,6},{8,9},{9,8},{10,11... | collective-permute-start | bytes 442376 | tf_op jit(solution)/shard_map/ppermute | solution.py:465
  75.8 76.8 %collective-permute-start.19 = (bf16[192,384]{1,0:T(8,128)(2,1)}, bf16[192,384]{1,0:T(8,128)(2,1)}, u32[]{:S(2)}, u32[]{:S(2)}) collective-permute-start(bf16[192,384]{1,0:T(8,128)(2,1)} %collective-permute-done.11.refs_9_), channel_id=1, source_target_pairs={{0,1},{1,0},{2,3},{3,2},{4,5},{5,4},{6,7},{7,6},{8,9},{9,8},{10,11... | collective-permute-start | bytes 442376 | tf_op jit(solution)/shard_map/ppermute | solution.py:465
  151.9 158.8 %collective-permute-start.116 = (bf16[2,384,768]{2,1,0:T(8,128)(2,1)}, bf16[2,384,768]{2,1,0:T(8,128)(2,1)}, u32[]{:S(2)}, u32[]{:S(2)}) collective-permute-start(bf16[2,384,768]{2,1,0:T(8,128)(2,1)} %get-tuple-element.70), channel_id=1, source_target_pairs={{0,1},{1,0},{2,3},{3,2},{4,5},{5,4},{6,7},{7,6},{8,9},{9,8},{10,11... | collective-permute-start | bytes 3538952 | tf_op jit(solution)/shard_map/ppermute | solution.py:465
  152.0 162.5 %collective-permute-start.98 = (bf16[2,384,768]{2,1,0:T(8,128)(2,1)}, bf16[2,384,768]{2,1,0:T(8,128)(2,1)S(1)}, u32[]{:S(2)}, u32[]{:S(2)}) collective-permute-start(bf16[2,384,768]{2,1,0:T(8,128)(2,1)} %get-tuple-element.64), channel_id=1, source_target_pairs={{0,1},{1,0},{2,3},{3,2},{4,5},{5,4},{6,7},{7,6},{8,9},{9,8},{10,11... | collective-permute-start | bytes 3538952 | tf_op jit(solution)/shard_map/ppermute | solution.py:465
  152.5 171.5 %collective-permute-start.104 = (bf16[2,384,768]{2,1,0:T(8,128)(2,1)}, bf16[2,384,768]{2,1,0:T(8,128)(2,1)S(1)}, u32[]{:S(2)}, u32[]{:S(2)}) collective-permute-start(bf16[2,384,768]{2,1,0:T(8,128)(2,1)} %get-tuple-element.66), channel_id=1, source_target_pairs={{0,1},{1,0},{2,3},{3,2},{4,5},{5,4},{6,7},{7,6},{8,9},{9,8},{10,11... | collective-permute-start | bytes 3538952 | tf_op jit(solution)/shard_map/ppermute | solution.py:465
  207.3 18.5 %collective-permute-start.86 = (bf16[384,768]{1,0:T(8,128)(2,1)S(1)}, bf16[384,768]{1,0:T(8,128)(2,1)S(1)}, u32[]{:S(2)}, u32[]{:S(2)}) collective-permute-start(bf16[384,768]{1,0:T(8,128)(2,1)S(1)} %constant_dynamic-slice_fusion.12), channel_id=1, source_target_pairs={{0,1},{1,0},{2,3},{3,2},{4,5},{5,4},{6,7},{7,6},{8,9},{9,8},{10,11... | collective-permute-start | bytes 1769480 | tf_op jit(solution)/shard_map/ppermute | solution.py:465
  225.9 135.0 %collective-permute-start.110 = (bf16[2,384,768]{2,1,0:T(8,128)(2,1)S(1)}, bf16[2,384,768]{2,1,0:T(8,128)(2,1)S(1)}, u32[]{:S(2)}, u32[]{:S(2)}) collective-permute-start(bf16[2,384,768]{2,1,0:T(8,128)(2,1)S(1)} %copy-done.54), channel_id=1, source_target_pairs={{0,1},{1,0},{2,3},{3,2},{4,5},{5,4},{6,7},{7,6},{8,9},{9,8},{10,11... | collective-permute-start | bytes 3538952 | tf_op jit(solution)/shard_map/ppermute | solution.py:465
  310.7 6.9 %collective-permute-start.55 = (bf16[96,768]{1,0:T(8,128)(2,1)S(1)}, bf16[96,768]{1,0:T(8,128)(2,1)S(1)}, u32[]{:S(2)}, u32[]{:S(2)}) collective-permute-start(bf16[96,768]{1,0:T(8,128)(2,1)S(1)} %pad_maximum_fusion.5), channel_id=1, source_target_pairs={{0,2},{2,0},{4,6},{6,4},{1,3},{3,1},{5,7},{7,5},{8,10},{10,8},{12,... | collective-permute-start | bytes 442376 | tf_op jit(solution)/shard_map/ppermute | solution.py:465
  317.6 33.5 %collective-permute-start.117 = (bf16[192,768]{1,0:T(8,128)(2,1)S(1)}, bf16[192,768]{1,0:T(8,128)(2,1)S(1)}, u32[]{:S(2)}, u32[]{:S(2)}) collective-permute-start(bf16[192,768]{1,0:T(8,128)(2,1)S(1)} %dynamic-slice_bitcast_fusion.1), channel_id=1, source_target_pairs={{0,8},{8,0},{16,24},{24,16},{1,9},{9,1},{17,25},{25,17},{2,10},{10... | collective-permute-start | bytes 884744 | tf_op jit(solution)/shard_map/ppermute | solution.py:465
  321.1 31.2 %collective-permute-start.119 = (bf16[192,768]{1,0:T(8,128)(2,1)S(1)}, bf16[192,768]{1,0:T(8,128)(2,1)S(1)}, u32[]{:S(2)}, u32[]{:S(2)}) collective-permute-start(bf16[192,768]{1,0:T(8,128)(2,1)S(1)} %dynamic-slice_bitcast_fusion), channel_id=1, source_target_pairs={{0,16},{8,24},{16,0},{24,8},{1,17},{9,25},{17,1},{25,9},{2,18},{10... | collective-permute-start | bytes 884744 | tf_op jit(solution)/shard_map/ppermute | solution.py:465
  322.6 31.2 %collective-permute-start.99 = (bf16[192,768]{1,0:T(8,128)(2,1)S(1)}, bf16[192,768]{1,0:T(8,128)(2,1)S(1)}, u32[]{:S(2)}, u32[]{:S(2)}) collective-permute-start(bf16[192,768]{1,0:T(8,128)(2,1)S(1)} %dynamic-slice_bitcast_fusion.7), channel_id=1, source_target_pairs={{0,8},{8,0},{16,24},{24,16},{1,9},{9,1},{17,25},{25,17},{2,10},{10... | collective-permute-start | bytes 884744 | tf_op jit(solution)/shard_map/ppermute | solution.py:465
  336.7 7.1 %collective-permute-start.68 = (bf16[96,768]{1,0:T(8,128)(2,1)S(1)}, bf16[96,768]{1,0:T(8,128)(2,1)S(1)}, u32[]{:S(2)}, u32[]{:S(2)}) collective-permute-start(bf16[96,768]{1,0:T(8,128)(2,1)S(1)} %fusion.4), channel_id=1, source_target_pairs={{0,4},{2,6},{4,0},{6,2},{1,5},{3,7},{5,1},{7,3},{8,12},{10,14},{12... | collective-permute-start | bytes 442376 | tf_op jit(solution)/shard_map/ppermute | solution.py:465
  350.0 9.9 %collective-permute-start.101 = (bf16[192,768]{1,0:T(8,128)(2,1)S(1)}, bf16[192,768]{1,0:T(8,128)(2,1)S(1)}, u32[]{:S(2)}, u32[]{:S(2)}) collective-permute-start(bf16[192,768]{1,0:T(8,128)(2,1)S(1)} %dynamic-slice_bitcast_fusion.6), channel_id=1, source_target_pairs={{0,16},{8,24},{16,0},{24,8},{1,17},{9,25},{17,1},{25,9},{2,18},{10... | collective-permute-start | bytes 884744 | tf_op jit(solution)/shard_map/ppermute | solution.py:465
  351.1 34.5 %collective-permute-start.105 = (bf16[192,768]{1,0:T(8,128)(2,1)S(1)}, bf16[192,768]{1,0:T(8,128)(2,1)S(1)}, u32[]{:S(2)}, u32[]{:S(2)}) collective-permute-start(bf16[192,768]{1,0:T(8,128)(2,1)S(1)} %dynamic-slice_bitcast_fusion.5), channel_id=1, source_target_pairs={{0,8},{8,0},{16,24},{24,16},{1,9},{9,1},{17,25},{25,17},{2,10},{10... | collective-permute-start | bytes 884744 | tf_op jit(solution)/shard_map/ppermute | solution.py:465
  352.3 34.4 %collective-permute-start.107 = (bf16[192,768]{1,0:T(8,128)(2,1)S(1)}, bf16[192,768]{1,0:T(8,128)(2,1)S(1)}, u32[]{:S(2)}, u32[]{:S(2)}) collective-permute-start(bf16[192,768]{1,0:T(8,128)(2,1)S(1)} %dynamic-slice_bitcast_fusion.4), channel_id=1, source_target_pairs={{0,16},{8,24},{16,0},{24,8},{1,17},{9,25},{17,1},{25,9},{2,18},{10... | collective-permute-start | bytes 884744 | tf_op jit(solution)/shard_map/ppermute | solution.py:465
  353.9 13.2 %collective-permute-start.93 = (bf16[48,768]{1,0:T(8,128)(2,1)S(1)}, bf16[48,768]{1,0:T(8,128)(2,1)S(1)}, u32[]{:S(2)}, u32[]{:S(2)}) collective-permute-start(bf16[48,768]{1,0:T(8,128)(2,1)S(1)} %get-tuple-element.114), channel_id=1, source_target_pairs={{0,16},{8,24},{16,0},{24,8},{1,17},{9,25},{17,1},{25,9},{2,18},{10... | collective-permute-start | bytes 221192 | tf_op jit(solution)/shard_map/ppermute | solution.py:465
  359.9 9.8 %collective-permute-start.95 = (bf16[48,768]{1,0:T(8,128)(2,1)S(1)}, bf16[48,768]{1,0:T(8,128)(2,1)S(1)}, u32[]{:S(2)}, u32[]{:S(2)}) collective-permute-start(bf16[48,768]{1,0:T(8,128)(2,1)S(1)} %get-tuple-element.115), channel_id=1, source_target_pairs={{0,8},{8,0},{16,24},{24,16},{1,9},{9,1},{17,25},{25,17},{2,10},{10... | collective-permute-start | bytes 221192 | tf_op jit(solution)/shard_map/ppermute | solution.py:465
  360.9 7.8 %collective-permute-start.57 = (bf16[48,768]{1,0:T(8,128)(2,1)S(1)}, bf16[48,768]{1,0:T(8,128)(2,1)S(1)}, u32[]{:S(2)}, u32[]{:S(2)}) collective-permute-start(bf16[48,768]{1,0:T(8,128)(2,1)S(1)} %get-tuple-element.116), channel_id=1, source_target_pairs={{0,16},{8,24},{16,0},{24,8},{1,17},{9,25},{17,1},{25,9},{2,18},{10... | collective-permute-start | bytes 221192 | tf_op jit(solution)/shard_map/ppermute | solution.py:465
  380.9 20.7 %collective-permute-start.111 = (bf16[192,768]{1,0:T(8,128)(2,1)S(1)}, bf16[192,768]{1,0:T(8,128)(2,1)S(1)}, u32[]{:S(2)}, u32[]{:S(2)}) collective-permute-start(bf16[192,768]{1,0:T(8,128)(2,1)S(1)} %dynamic-slice_bitcast_fusion.3), channel_id=1, source_target_pairs={{0,8},{8,0},{16,24},{24,16},{1,9},{9,1},{17,25},{25,17},{2,10},{10... | collective-permute-start | bytes 884744 | tf_op jit(solution)/shard_map/ppermute | solution.py:465
  382.5 19.3 %collective-permute-start.113 = (bf16[192,768]{1,0:T(8,128)(2,1)S(1)}, bf16[192,768]{1,0:T(8,128)(2,1)S(1)}, u32[]{:S(2)}, u32[]{:S(2)}) collective-permute-start(bf16[192,768]{1,0:T(8,128)(2,1)S(1)} %dynamic-slice_bitcast_fusion.2), channel_id=1, source_target_pairs={{0,16},{8,24},{16,0},{24,8},{1,17},{9,25},{17,1},{25,9},{2,18},{10... | collective-permute-start | bytes 884744 | tf_op jit(solution)/shard_map/ppermute | solution.py:465
  401.1 8.7 %collective-permute-start.103 = (bf16[2,96,768]{2,1,0:T(8,128)(2,1)S(1)}, bf16[2,96,768]{2,1,0:T(8,128)(2,1)S(1)}, u32[]{:S(2)}, u32[]{:S(2)}) collective-permute-start(bf16[2,96,768]{2,1,0:T(8,128)(2,1)S(1)} %pad_maximum_fusion.4), channel_id=1, source_target_pairs={{0,2},{2,4},{4,6},{6,0},{1,3},{3,5},{5,7},{7,1},{8,10},{10,12},{12... | collective-permute-start | bytes 884744 | tf_op jit(solution)/shard_map/ppermute | solution.py:470
  401.7 37.2 %collective-permute-start.97 = (bf16[384,768]{1,0:T(8,128)(2,1)S(1)}, bf16[384,768]{1,0:T(8,128)(2,1)S(1)}, u32[]{:S(2)}, u32[]{:S(2)}) collective-permute-start(bf16[384,768]{1,0:T(8,128)(2,1)S(1)} %pad_maximum_fusion.3), channel_id=1, source_target_pairs={{0,1},{1,0},{2,3},{3,2},{4,5},{5,4},{6,7},{7,6},{8,9},{9,8},{10,11... | collective-permute-start | bytes 1769480 | tf_op jit(solution)/shard_map/ppermute | solution.py:465
  401.8 17.7 %collective-permute-start.61 = (bf16[384,768]{1,0:T(8,128)(2,1)S(1)}, bf16[384,768]{1,0:T(8,128)(2,1)S(1)}, u32[]{:S(2)}, u32[]{:S(2)}) collective-permute-start(bf16[384,768]{1,0:T(8,128)(2,1)S(1)} %pad_maximum_fusion), channel_id=1, source_target_pairs={{0,1},{1,0},{2,3},{3,2},{4,5},{5,4},{6,7},{7,6},{8,9},{9,8},{10,11... | collective-permute-start | bytes 1769480 | tf_op jit(solution)/shard_map/ppermute | solution.py:465
  402.7 17.3 %collective-permute-start.73 = (bf16[384,768]{1,0:T(8,128)(2,1)S(1)}, bf16[384,768]{1,0:T(8,128)(2,1)S(1)}, u32[]{:S(2)}, u32[]{:S(2)}) collective-permute-start(bf16[384,768]{1,0:T(8,128)(2,1)S(1)} %pad_maximum_fusion.1), channel_id=1, source_target_pairs={{0,1},{1,0},{2,3},{3,2},{4,5},{5,4},{6,7},{7,6},{8,9},{9,8},{10,11... | collective-permute-start | bytes 1769480 | tf_op jit(solution)/shard_map/ppermute | solution.py:465
  410.9 8.6 %collective-permute-start.109 = (bf16[2,96,768]{2,1,0:T(8,128)(2,1)S(1)}, bf16[2,96,768]{2,1,0:T(8,128)(2,1)S(1)}, u32[]{:S(2)}, u32[]{:S(2)}) collective-permute-start(bf16[2,96,768]{2,1,0:T(8,128)(2,1)S(1)} %maximum_add_fusion), channel_id=1, source_target_pairs={{0,2},{2,4},{4,6},{6,0},{1,3},{3,5},{5,7},{7,1},{8,10},{10,12},{12... | collective-permute-start | bytes 884744 | tf_op jit(solution)/shard_map/ppermute | solution.py:470
  415.0 14.3 %collective-permute-start.85 = (bf16[384,768]{1,0:T(8,128)(2,1)S(1)}, bf16[384,768]{1,0:T(8,128)(2,1)S(1)}, u32[]{:S(2)}, u32[]{:S(2)}) collective-permute-start(bf16[384,768]{1,0:T(8,128)(2,1)S(1)} %pad_maximum_fusion.2), channel_id=1, source_target_pairs={{0,1},{1,0},{2,3},{3,2},{4,5},{5,4},{6,7},{7,6},{8,9},{9,8},{10,11... | collective-permute-start | bytes 1769480 | tf_op jit(solution)/shard_map/ppermute | solution.py:465
  419.5 8.6 %collective-permute-start.115 = (bf16[2,96,768]{2,1,0:T(8,128)(2,1)S(1)}, bf16[2,96,768]{2,1,0:T(8,128)(2,1)S(1)}, u32[]{:S(2)}, u32[]{:S(2)}) collective-permute-start(bf16[2,96,768]{2,1,0:T(8,128)(2,1)S(1)} %maximum_add_fusion.1), channel_id=1, source_target_pairs={{0,2},{2,4},{4,6},{6,0},{1,3},{3,5},{5,7},{7,1},{8,10},{10,12},{12... | collective-permute-start | bytes 884744 | tf_op jit(solution)/shard_map/ppermute | solution.py:470
  429.7 8.0 %collective-permute-start.121 = (bf16[96,768]{1,0:T(8,128)(2,1)S(1)}, bf16[96,768]{1,0:T(8,128)(2,1)S(1)}, u32[]{:S(2)}, u32[]{:S(2)}) collective-permute-start(bf16[96,768]{1,0:T(8,128)(2,1)S(1)} %get-tuple-element.113), channel_id=1, source_target_pairs={{0,16},{8,24},{16,0},{24,8},{1,17},{9,25},{17,1},{25,9},{2,18},{10... | collective-permute-start | bytes 442376 | tf_op jit(solution)/shard_map/ppermute | solution.py:465
  433.4 7.1 %collective-permute-start.124 = (bf16[192,768]{1,0:T(8,128)(2,1)S(1)}, bf16[192,768]{1,0:T(8,128)(2,1)S(1)}, u32[]{:S(2)}, u32[]{:S(2)}) collective-permute-start(bf16[192,768]{1,0:T(8,128)(2,1)S(1)} %maximum_select_fusion.15), channel_id=1, source_target_pairs={{0,16},{8,24},{16,0},{24,8},{1,17},{9,25},{17,1},{25,9},{2,18},{10... | collective-permute-start | bytes 884744 | tf_op jit(solution)/shard_map/ppermute | solution.py:465
  437.8 6.8 %collective-permute-start.122 = (bf16[192,768]{1,0:T(8,128)(2,1)S(1)}, bf16[192,768]{1,0:T(8,128)(2,1)S(1)}, u32[]{:S(2)}, u32[]{:S(2)}) collective-permute-start(bf16[192,768]{1,0:T(8,128)(2,1)S(1)} %maximum_select_fusion.14), channel_id=1, source_target_pairs={{0,8},{8,0},{16,24},{24,16},{1,9},{9,1},{17,25},{25,17},{2,10},{10... | collective-permute-start | bytes 884744 | tf_op jit(solution)/shard_map/ppermute | solution.py:465
  (137 other events, 2189.9 us)
